TPU v7x, 32 devices: a whole 2x2x4 slice. The times are simulated.
32 devices in a mesh: freq: 4 (over z), src: 8 (over y, x, core).
Axes of the slice: x: 2, y: 2, z: 4, core: 2. Of those that a mesh axis runs over, the one named last changes fastest.
Arguments:
- data: bfloat16 [2, 4, 128, 24576], P(None, 'freq', None, 'src'), may hold values from -6 to 6
- recip: bfloat16 [2, 4, 128, 128], P(None, 'freq', None, 'src'), may hold values from -6 to 6
- gap: int32 [128, 128], P(None, 'src'), may hold values 0 or 1
- owner: int32 [8], replicated, may hold values from 0 to 7, as said below
- weights: bfloat16 [2, 4, 24576, 64], P(None, 'freq', 'src'), may hold values from -0.0390625 to 0.0390625
- start_row: int32 [4], P('freq'), may hold values from 0 to 96, as said below
- end_row: int32 [4], P('freq'), may hold values from 32 to 128, as said below
- recorded: bfloat16 [192, 64, 128], P('freq', 'src'), may hold values from -6 to 6
Outputs:
- primaries: bfloat16 [192, 64, 128], P('freq', 'src')
- filters: float32 [4, 27], P('freq')
Inputs may be any that keep to these rules, and one draw needn't show every extreme that they name: `owner`: a permutation: each block is named by exactly one src index. `start_row`: start of window i lies between i * 32 - 8 and i * 32, never before 0; window 1 starts exactly 8 early. `end_row`: end of window i lies between (i + 1) * 32 and (i + 1) * 32 + 8, never after 128; window 1 ends exactly 8 late.
All inputs are finite; a program needn't handle non-finite values. No bound on the sum of `gap` on one device may be relied on, other than what follows from the above.
Results may differ from a plain program's by a relative error of at most 0.001.
Values may be sent and summed in bfloat16 or wider, within the bound.
A program may use at most 64 MiB of HBM per device.

v0:
```python
import math

import jax
import jax.numpy as jnp
from jax import lax
from jax.sharding import PartitionSpec as P

RECV = 128
NFFT = 512
F_LOW = 40
NEAR = 16
HALO = 8
LAGS_T = 9
LAGS_X = 3


def padded_2(array, sides, width):
    for axis, dim in sides:
        devices, length = (lax.axis_size(axis), array.shape[dim])
        up = [(i, (i + 1) % devices) for i in range(devices - 1)]
        down = [(j, i) for i, j in up]
        last = lax.slice_in_dim(array, length - width, length, axis=dim)
        leading = lax.slice_in_dim(array, 0, width, axis=dim)
        before = lax.ppermute(last, axis, up)
        after = lax.ppermute(leading, axis, down)
        array = jnp.concatenate([before, array, after], axis=dim)
    return array


def phase_tables(times, freqs):
    turns = (F_LOW + freqs)[None, :] * times[:, None] % NFFT
    angle = turns.astype(jnp.float32) * (2.0 * math.pi / NFFT)
    return (jnp.cos(angle), jnp.sin(angle))


def shifted_stack(masked, keep):
    lead = LAGS_T // 2
    side = LAGS_X // 2
    padded = jnp.pad(masked, ((lead, lead), (0, 0), (side, side)))
    height = masked.shape[0]
    width = masked.shape[2]
    pieces = [
        padded[LAGS_T - 1 - a : LAGS_T - 1 - a + height, :, LAGS_X - 1 - b : LAGS_X - 1 - b + width]
        for a in range(LAGS_T)
        for b in range(LAGS_X)
    ]
    return jnp.stack(pieces) * keep[None, :, None, None]


def solve_filter(gram, rhs, damping):
    count = gram.shape[0]
    centre = LAGS_T // 2 * LAGS_X + LAGS_X // 2
    unit = (jnp.arange(count) == centre).astype(jnp.float32)
    eye = jnp.eye(count, dtype=jnp.float32)
    factor = jnp.linalg.cholesky(gram + damping * eye)
    return jax.scipy.linalg.cho_solve((factor, True), rhs + damping * unit)


def body(data, recip, gap, owner, weights, start_row, end_row, recorded):
    hp = lax.Precision.HIGHEST
    src_here = lax.axis_index("src")
    freq_here = lax.axis_index("freq")
    src_count = lax.axis_size("src")
    freq_count = lax.axis_size("freq")
    nfreq_local = data.shape[1]
    total_freq = nfreq_local * freq_count
    total_out = weights.shape[3]
    out_local = total_out // src_count
    block_rows = recorded.shape[0] - 2 * HALO
    total_time = block_rows * freq_count
    scale = 1.0 / math.sqrt(total_freq)
    piece = lax.all_gather(recip, "src", axis=3, tiled=True)
    count = piece.shape[3] // NEAR
    select = (owner == src_here).astype(jnp.float32)
    split = piece.reshape(2, nfreq_local, RECV, count, NEAR).astype(jnp.float32)
    filled = jnp.einsum("cfrqn,q->cfrn", split, select)
    near = jnp.where((gap == 1)[None, None], filled.astype(jnp.bfloat16), data[..., :NEAR])
    panel = jnp.concatenate([near, data[..., NEAR:]], axis=3)
    real = jnp.einsum(
        "frk,fks->sfr", panel[0], weights[0], preferred_element_type=jnp.float32
    ) - jnp.einsum("frk,fks->sfr", panel[1], weights[1], preferred_element_type=jnp.float32)
    imag = jnp.einsum(
        "frk,fks->sfr", panel[0], weights[1], preferred_element_type=jnp.float32
    ) + jnp.einsum("frk,fks->sfr", panel[1], weights[0], preferred_element_type=jnp.float32)
    summed = lax.psum(jnp.stack([real, imag], axis=1), "src")
    local_pred = lax.dynamic_slice_in_dim(summed, src_here * out_local, out_local, 0)
    spread = lax.all_to_all(local_pred, "freq", split_axis=3, concat_axis=2, tiled=True)
    cosine, sine = phase_tables(
        jnp.arange(total_time, dtype=jnp.int32), jnp.arange(total_freq, dtype=jnp.int32)
    )
    series = (
        jnp.einsum("tf,sfr->tsr", cosine, spread[:, 0], precision=hp)
        - jnp.einsum("tf,sfr->tsr", sine, spread[:, 1], precision=hp)
    ) * scale
    block = lax.all_to_all(series, "freq", split_axis=0, concat_axis=2, tiled=True)
    ext = padded_2(block, (("freq", 0),), HALO)
    rows = freq_here * block_rows - HALO + jnp.arange(recorded.shape[0], dtype=jnp.int32)
    keep = ((rows >= start_row[0]) & (rows < end_row[0])).astype(jnp.float32)
    target = recorded.astype(jnp.float32) * keep[:, None, None]
    stack = shifted_stack(ext * keep[:, None, None], keep)
    flat = stack.reshape(stack.shape[0], -1)
    gram = jnp.dot(flat, flat.T, precision=hp)
    rhs = jnp.dot(flat, target.reshape(-1), precision=hp)
    gram, rhs = lax.psum((gram, rhs), "src")
    damping = float(recorded.shape[0] * total_out * RECV)
    filt = solve_filter(gram, rhs, damping)
    matched = jnp.einsum("u,uwsr->wsr", filt, stack, precision=hp)
    primaries = (target - matched).astype(jnp.bfloat16)
    return (primaries, filt[None, :])


def solution(mesh):
    placed = (
        P(None, "freq", None, "src"),
        P(None, "freq", None, "src"),
        P(None, "src"),
        P(),
        P(None, "freq", "src", None),
        P("freq"),
        P("freq"),
        P("freq", "src", None),
    )
    return jax.shard_map(
        body,
        mesh=mesh,
        in_specs=placed,
        out_specs=(P("freq", "src", None), P("freq", None)),
        check_vma=False,
    )
```

profile of v0, /device:TPU:0, one launch (start us, length us, event | category | flops | bytes accessed | tf_op | source)
XLA Modules:
  0.0 178.4 jit_solution(7545261546091947731)
XLA Ops:
  7.2 0.8 broadcast_compare_fusion
  8.1 10.7 %all_gather.3 = bf16[2,1,128,128]{2,3,1,0:T(8,128)(2,1)S(1)} all-gather(bf16[2,1,128,16]{2,3,1,0:T(8,128)(2,1)} %param.9), channel_id=1, replica_groups=mesh['freq'=4,'src'=8] {'src'}, dimensions={3}, use_global_device_ids=true | all-gather | bytes 73728 | tf_op jit(solution)/shard_map/all_gather | solution.py:72
  18.8 0.8 fusion.85
  19.7 2.0 %slice.138 = bf16[2,1,128,3056]{3,2,1,0:T(8,128)(2,1)S(1)} slice(bf16[2,1,128,3072]{3,2,1,0:T(8,128)(2,1)} %param.8), slice={[0:2], [0:1], [0:128], [16:3072]} | slice | bytes 3129344 | tf_op jit(solution)/shard_map/slice | solution.py:78
  21.7 0.9 fusion.84
  22.6 1.5 fusion.18
  26.3 52.8 %all-reduce.4.cloned.1.call-done = f32[64,2,1,128]{3,0,2,1:T(8,128)} async-done(((f32[64,2,1,128]{3,0,2,1:T(8,128)}), f32[64,2,1,128]{3,0,2,1:T(8,128)}) %all-reduce.4.cloned.1.call-update) | async-done | bytes 65552 | tf_op jit(solution)/shard_map/psum | solution.py:85
  80.5 1.0 reduce.6
  81.4 0.8 reshape.158
  82.2 4.6 %all-to-all-start = ((f32[4,1,512]{2,1,0:T(1,128)}), f32[4,1,512]{2,1,0:T(1,128)S(1)}, u32[]{:S(2)}, u32[]{:S(2)}) async-start(f32[4,1,512]{2,1,0:T(1,128)} %reshape.158), calls=%async_computation | async-start | bytes 16384 | tf_op jit(solution)/shard_map/all_to_all | solution.py:87
  86.8 5.6 %all-to-all-done = f32[4,1,512]{2,1,0:T(1,128)S(1)} async-done(((f32[4,1,512]{2,1,0:T(1,128)}), f32[4,1,512]{2,1,0:T(1,128)S(1)}, u32[]{:S(2)}, u32[]{:S(2)}) %all-to-all-start) | async-done | bytes 8224 | tf_op jit(solution)/shard_map/all_to_all | solution.py:87
  94.7 0.9 reshape.160
  95.6 3.3 %all-to-all-start.1 = ((f32[4,1,8192]{2,1,0:T(1,128)}), f32[4,1,8192]{2,1,0:T(1,128)S(1)}, u32[]{:S(2)}, u32[]{:S(2)}) async-start(f32[4,1,8192]{2,1,0:T(1,128)} %reshape.160), calls=%async_computation.1 | async-start | bytes 262144 | tf_op jit(solution)/shard_map/all_to_all | solution.py:95
  100.2 4.6 %all-to-all-done.1 = f32[4,1,8192]{2,1,0:T(1,128)S(1)} async-done(((f32[4,1,8192]{2,1,0:T(1,128)}), f32[4,1,8192]{2,1,0:T(1,128)S(1)}, u32[]{:S(2)}, u32[]{:S(2)}) %all-to-all-start.1) | async-done | bytes 131104 | tf_op jit(solution)/shard_map/all_to_all | solution.py:95
  104.8 0.9 reduce.8
  106.1 3.2 %collective-permute-start = (f32[8,8,128]{2,1,0:T(8,128)S(1)}, f32[8,8,128]{2,1,0:T(8,128)S(1)}, u32[]{:S(2)}, u32[]{:S(2)}) collective-permute-start(f32[8,8,128]{2,1,0:T(8,128)S(1)} %slice.146), channel_id=1, source_target_pairs={{0,8},{8,16},{16,24},{1,9},{9,17},{17,25},{2,10},{10,18},{18,26},{... | collective-permute-start | bytes 98312 | tf_op jit(solution)/shard_map/ppermute | solution.py:24
  109.5 1.5 collective-permute-start.1
  111.9 3.4 %collective-permute-done.1 = f32[8,8,128]{2,1,0:T(8,128)S(1)} collective-permute-done((f32[8,8,128]{2,1,0:T(8,128)S(1)}, f32[8,8,128]{2,1,0:T(8,128)S(1)}, u32[]{:S(2)}, u32[]{:S(2)}) %collective-permute-start.1) | collective-permute-done | bytes 32800 | tf_op jit(solution)/shard_map/ppermute | solution.py:25
  118.6 7.2 %fusion.9 = f32[27,27]{1,0:T(8,128)S(1)} fusion(f32[27,48,8,128]{3,2,1,0:T(8,128)S(1)} %broadcast_multiply_fusion), kind=kOutput, calls=%fused_computation.41 | convolution fusion | flops 429981696 | bytes 5311332 | tf_op jit(solution)/shard_map/dot_general | solution.py:102
  125.9 7.6 %fusion.12 = f32[27]{0:T(128)S(1)} fusion(f32[48,8,128,1]{2,3,1,0:T(1,128)S(1)} %bitcast.214, f32[27,48,8,128]{3,2,1,0:T(8,128)S(1)} %broadcast_multiply_fusion), kind=kOutput, calls=%fused_computation.43 | convolution fusion | flops 15925248 | bytes 5505132 | tf_op jit(solution)/shard_map/dot_general | solution.py:103
  133.4 22.4 %all-reduce.1 = (f32[27,27]{1,0:T(8,128)S(1)}, f32[27]{0:T(128)S(1)}) all-reduce(f32[27,27]{1,0:T(8,128)S(1)} %fusion.9, f32[27]{0:T(128)S(1)} %fusion.12), channel_id=1, replica_groups=mesh['freq'=4,'src'=8] {'src'}, use_global_device_ids=true, to_apply=%region_1.2 | all-reduce | flops 756 | bytes 6048 | tf_op jit(solution)/shard_map/psum | solution.py:104
  155.9 2.5 %cholesky.16 = f32[27,27]{1,0:T(8,128)S(1)} custom-call(f32[27,27]{1,0:T(8,128)S(1)} %fusion.91), custom_call_target="Cholesky" | custom-call | tf_op jit(solution)/shard_map/jit(cholesky)/cholesky | solution.py:55
  159.7 2.1 %custom-call.10 = f32[1,27,27]{1,2,0:T(8,128)S(1)} custom-call(f32[1,27,27]{2,1,0:T(8,128)S(1)} %fusion.87), custom_call_target="InvertDiagBlocksLowerTriangular" | custom-call | tf_op jit(solution)/shard_map/jit(_cho_solve)/triangular_solve | solution.py:56
  162.1 8.7 %fusion = f32[1,48,8,128]{3,0,2,1:T(1,128)S(1)} fusion(f32[27,48,8,128]{3,2,1,0:T(8,128)} %copy-done, f32[1,27]{1,0:T(1,128)S(1)} %fusion.88), kind=kOutput, calls=%fused_computation | convolution fusion | flops 15925248 | bytes 5505132 | tf_op jit(solution)/shard_map/u,uwsr->wsr/dot_general | solution.py:107
  (77 shorter events, 13.1 us)
Async XLA Ops:
  7.2 16.9 %copy-start.1 = (bf16[2,1,3072,64]{2,3,1,0:T(8,128)(2,1)S(1)}, bf16[2,1,3072,64]{2,3,1,0:T(8,128)(2,1)}, u32[]{:S(2)}) copy-start(bf16[2,1,3072,64]{2,3,1,0:T(8,128)(2,1)} %param.12) | copy-start | bytes 2359300
  7.2 71.9 %all-reduce.4.cloned.1.call-start = ((), (), s32[]{:S(2)}) async-start(), calls=%async_computation.2 | async-start | bytes 131072 | tf_op jit(solution)/shard_map/psum | solution.py:85
  25.1 90.2 %copy-start.2 = (bf16[48,8,128]{2,1,0:T(8,128)(2,1)S(1)}, bf16[48,8,128]{2,1,0:T(8,128)(2,1)}, u32[]{:S(2)}) copy-start(bf16[48,8,128]{2,1,0:T(8,128)(2,1)} %param.15) | copy-start | bytes 294916
  82.2 10.2 %all-to-all-start = ((f32[4,1,512]{2,1,0:T(1,128)}), f32[4,1,512]{2,1,0:T(1,128)S(1)}, u32[]{:S(2)}, u32[]{:S(2)}) async-start(f32[4,1,512]{2,1,0:T(1,128)} %reshape.158), calls=%async_computation | async-start | bytes 16384 | tf_op jit(solution)/shard_map/all_to_all | solution.py:87
  95.6 9.2 %all-to-all-start.1 = ((f32[4,1,8192]{2,1,0:T(1,128)}), f32[4,1,8192]{2,1,0:T(1,128)S(1)}, u32[]{:S(2)}, u32[]{:S(2)}) async-start(f32[4,1,8192]{2,1,0:T(1,128)} %reshape.160), calls=%async_computation.1 | async-start | bytes 262144 | tf_op jit(solution)/shard_map/all_to_all | solution.py:95
  106.1 5.8 %collective-permute-start = (f32[8,8,128]{2,1,0:T(8,128)S(1)}, f32[8,8,128]{2,1,0:T(8,128)S(1)}, u32[]{:S(2)}, u32[]{:S(2)}) collective-permute-start(f32[8,8,128]{2,1,0:T(8,128)S(1)} %slice.146), channel_id=1, source_target_pairs={{0,8},{8,16},{16,24},{1,9},{9,17},{17,25},{2,10},{10,18},{18,26},{... | collective-permute-start | bytes 98312 | tf_op jit(solution)/shard_map/ppermute | solution.py:24
  109.5 5.8 %collective-permute-start.1 = (f32[8,8,128]{2,1,0:T(8,128)S(1)}, f32[8,8,128]{2,1,0:T(8,128)S(1)}, u32[]{:S(2)}, u32[]{:S(2)}) collective-permute-start(f32[8,8,128]{2,1,0:T(8,128)S(1)} %slice.148), channel_id=1, source_target_pairs={{8,0},{16,8},{24,16},{9,1},{17,9},{25,17},{10,2},{18,10},{26,18},{... | collective-permute-start | bytes 98312 | tf_op jit(solution)/shard_map/ppermute | solution.py:25
  118.6 7.2 %copy-start = (f32[27,48,8,128]{3,2,1,0:T(8,128)}, f32[27,48,8,128]{3,2,1,0:T(8,128)S(1)}, u32[]{:S(2)}) copy-start(f32[27,48,8,128]{3,2,1,0:T(8,128)S(1)} %broadcast_multiply_fusion) | copy-start | bytes 15925252
  162.1 9.5 %copy-start.3 = (f32[1,27]{1,0:T(1,128)}, f32[1,27]{1,0:T(1,128)S(1)}, u32[]{:S(2)}) copy-start(f32[1,27]{1,0:T(1,128)S(1)} %fusion.88) | copy-start | bytes 328
Sparse Core Ops, SparseCore 0:
  26.5 52.5 all-reduce.3
where the time goes:
time: 179 us; the launch traced here: 178 us
  waiting for transfers between devices  66.4 us (37%)
  blocking collectives  33 us (18%)
  matrix products  28.6 us (16%)
  between operations  15.8 us (9%)
  starting transfers between devices  12.6 us (7%)
  other arithmetic  12.3 us (7%)
  local copies, waits for them, and re-layouts  9.71 us (5%)
    psum x1, waiting for transfers between devices, body(): summed = lax.psum(jnp.stack([real, imag], axis=1), 'src')  52.8 us
    psum x1, blocking collectives, body(): gram, rhs = lax.psum((gram, rhs), 'src')  22.4 us
    all_gather x1, blocking collectives, body(): piece = lax.all_gather(recip, 'src', axis=3, tiled=True)  10.7 us
    dot_general x1, matrix products, body(): matched = jnp.einsum('u,uwsr->wsr', filt, stack, precision=hp)  8.74 us
    dot_general x1, matrix products, body(): rhs = jnp.dot(flat, target.reshape(-1), precision=hp)  7.55 us
    dot_general x1, matrix products, body(): gram = jnp.dot(flat, flat.T, precision=hp)  7.22 us
    all_to_all x1, waiting for transfers between devices, body(): lax.all_to_all(local_pred, 'freq', split_axis=3, concat_axis=2, tiled=True)  5.59 us
    unnamed x40, local copies, waits for them, and re-layouts  4.79 us
  transfers between devices with their start and end apart: 5, of which 4 were waited for; matrix products, arithmetic and copies ran while one was open for 0% of the time, Pallas kernels for 0%

commit v1 on v0

v1 whole, which is shorter than its diff:
```python
import functools
import math

import jax
import jax.numpy as jnp
from jax import lax
from jax.experimental import pallas as pl
from jax.experimental.pallas import tpu as pltpu
from jax.sharding import PartitionSpec as P

RECV = 128
NFFT = 512
F_LOW = 40
NEAR = 16
HALO = 8
LAGS_T = 9
LAGS_X = 3
NU = LAGS_T * LAGS_X
NP = 32
CHUNKS = 4
F32 = jnp.float32
BF16 = jnp.bfloat16


def hdot(a, b, dims=((1,), (0,))):
    return lax.dot_general(
        a, b, (dims, ((), ())), precision=lax.Precision.HIGHEST, preferred_element_type=F32
    )


def bdot(a, b):
    return jnp.dot(a, b, preferred_element_type=F32)


def iota(shape, dim):
    return lax.broadcasted_iota(jnp.int32, shape, dim)


def third(n):
    return (n * 171) >> 9


def kernel(
    nsrc, nfreq, comps, total_out, scale,
    data, recip, gap, owner, weights, start, end, recorded,
    prim, filt,
    dbuf, wbuf, rin, gin, recb, rbuf, pout, pbuf, gath, shifts, rec32, zbuf, hbig,
    lsem, dsem, rsend, rrecv, psend, precv, gsend, grecv, zsend, zrecv,
):
    me = lax.axis_index("src")
    here = lax.axis_index("freq")
    depth = data.shape[3]
    wrows = recorded.shape[0]
    outs = recorded.shape[1]
    step = depth // CHUNKS
    sout = total_out
    log_c = comps.bit_length() - 1
    k3 = LAGS_X * comps

    local = [
        pltpu.make_async_copy(recip, rin, lsem.at[0]),
        pltpu.make_async_copy(gap, gin, lsem.at[1]),
        pltpu.make_async_copy(recorded, recb, lsem.at[2]),
    ]
    for copy in local:
        copy.start()
    big = []
    for i in range(CHUNKS):
        cut = pl.ds(i * step, step)
        big.append(
            (
                pltpu.make_async_copy(data.at[:, :, :, cut], dbuf.at[:, :, :, cut], dsem.at[2 * i]),
                pltpu.make_async_copy(weights.at[:, :, cut, :], wbuf.at[:, :, cut, :], dsem.at[2 * i + 1]),
            )
        )
        for copy in big[-1]:
            copy.start()

    src_peers = [lax.rem(me + k, nsrc) for k in range(1, nsrc)]
    freq_peers = [lax.rem(here + k, nfreq) for k in range(1, nfreq)]
    barrier = pltpu.get_barrier_semaphore()
    for peer in src_peers:
        pl.semaphore_signal(barrier, inc=1, device_id={"src": peer}, device_id_type=pl.DeviceIdType.MESH)
    for peer in freq_peers:
        pl.semaphore_signal(barrier, inc=1, device_id={"freq": peer}, device_id_type=pl.DeviceIdType.MESH)

    def exchange(axis, mine, peers, src_of, buf, rows, send, recv):
        slot = buf.at[pl.ds(pl.multiple_of(mine * rows, rows), rows), :]
        copies = []
        for k, peer in enumerate(peers):
            copies.append(
                pltpu.make_async_remote_copy(
                    src_ref=src_of(peer),
                    dst_ref=slot,
                    send_sem=send.at[k],
                    recv_sem=recv.at[k],
                    device_id={axis: peer},
                    device_id_type=pl.DeviceIdType.MESH,
                )
            )
            copies[-1].start()
        return copies

    local[0].wait()
    for i in range(2):
        flipped = rin[i, 0].astype(F32).T.astype(BF16)
        rbuf[pl.ds(pl.multiple_of(me * 2 * NEAR + i * NEAR, NEAR), NEAR), :] = flipped
    pl.semaphore_wait(barrier, nsrc - 1 + nfreq - 1)
    own = rbuf.at[pl.ds(pl.multiple_of(me * 2 * NEAR, 2 * NEAR), 2 * NEAR), :]
    sent_r = exchange("src", me, src_peers, lambda peer: own, rbuf, 2 * NEAR, rsend, rrecv)

    local[1].wait()
    missing = gin[...] == 1
    gap_t = jnp.where(missing, 1.0, 0.0).astype(F32).T
    acc0 = jnp.zeros((2 * RECV, sout), F32)
    acc1 = jnp.zeros((2 * RECV, sout), F32)
    for i in range(CHUNKS):
        for copy in big[i]:
            copy.wait()
        if i == 0:
            for ci in range(2):
                head = dbuf[ci, 0, :, :NEAR].astype(F32)
                dbuf[ci, 0, :, :NEAR] = jnp.where(missing, 0.0, head).astype(BF16)
        cut = slice(i * step, (i + 1) * step)
        left = dbuf[:, 0, :, cut].reshape(2 * RECV, step)
        acc0 = acc0 + bdot(left, wbuf[0, 0, cut, :])
        acc1 = acc1 + bdot(left, wbuf[1, 0, cut, :])
    real = (acc0[:RECV] - acc1[RECV:]).T
    imag = (acc1[:RECV] + acc0[RECV:]).T

    near_w = [wbuf[ci, 0, :NEAR, :].astype(F32).T.astype(BF16) for ci in range(2)]
    for copy in sent_r:
        copy.wait()
    near = []
    for ci in range(2):
        total = jnp.zeros((NEAR, RECV), F32)
        for j in range(nsrc):
            pick = jnp.where(owner[j] == me, 1.0, 0.0).astype(F32)
            total = total + rbuf[j * 2 * NEAR + ci * NEAR : j * 2 * NEAR + (ci + 1) * NEAR, :].astype(F32) * pick
        near.append((total * gap_t).astype(BF16))
    real = real + bdot(near_w[0], near[0]) - bdot(near_w[1], near[1])
    imag = imag + bdot(near_w[0], near[1]) + bdot(near_w[1], near[0])

    span = 2 * outs
    for d in range(nsrc):
        pout[d * span : d * span + outs, :] = real[d * outs : (d + 1) * outs]
        pout[d * span + outs : (d + 1) * span, :] = imag[d * outs : (d + 1) * outs]

    def block_for(peer):
        return pout.at[pl.ds(pl.multiple_of(peer * span, span), span), :]

    sent_p = exchange("src", me, src_peers, block_for, pbuf, span, psend, precv)
    mine = pl.ds(pl.multiple_of(me * span, span), span)
    pbuf[mine, :] = pout[mine, :]

    base = here * (wrows - 2 * HALO) - HALO
    first, last = start[0], end[0]

    def delayed(u, c, n):
        t = base + u
        v = t - (third(n) - LAGS_T // 2)
        valid = (t >= first) & (t < last) & (v >= first) & (v < last) & (n < NU)
        turns = ((F_LOW + (c >> 1)) * v + (NFFT // 4) * (c & 1)) & (NFFT - 1)
        return jnp.where(valid, jnp.cos(turns.astype(F32) * (2.0 * math.pi / NFFT)) * scale, 0.0)

    rows_cn = comps * NP
    shape = (rows_cn, 128)
    row = iota(shape, 0)
    u_t = delayed(iota(shape, 1), row >> 5, row & (NP - 1))
    shape = (wrows, rows_cn)
    lane = iota(shape, 1)
    u_n = delayed(iota(shape, 0), lane >> 5, lane & (NP - 1))
    shape = (128, 128)
    for c in range(comps):
        block = delayed(iota(shape, 0), c, iota(shape, 1))
        hbig[:, c * 128 : (c + 1) * 128] = hdot(u_t, block)
    shape = (rows_cn, k3)
    row, lane = iota(shape, 0), iota(shape, 1)
    n = row & (NP - 1)
    same = ((lane >> log_c) == n - 3 * third(n)) & ((lane & (comps - 1)) == (row >> 5)) & (n < NU)
    pick_rows = jnp.where(same, 1.0, 0.0).astype(F32)

    local[2].wait()
    rec32[...] = recb[...].astype(F32).reshape(wrows * outs, RECV)

    for copy in sent_p:
        copy.wait()
    pred = pbuf[0:span, :]
    for j in range(1, nsrc):
        pred = pred + pbuf[j * span : (j + 1) * span, :]
    mine = pl.ds(pl.multiple_of(here * span, span), span)
    gath[mine, :] = pred
    sent_g = exchange("freq", here, freq_peers, lambda peer: gath.at[mine, :], gath, span, gsend, grecv)
    for copy in sent_g:
        copy.wait()

    size = comps * outs
    whole = gath[...]
    lane = iota((size, RECV), 1)
    shifts[0:size, :] = jnp.where(lane == RECV - 1, 0.0, pltpu.roll(whole, RECV - 1, 1))
    shifts[size : 2 * size, :] = whole
    shifts[2 * size :, :] = jnp.where(lane == 0, 0.0, pltpu.roll(whole, 1, 1))
    waves = jnp.concatenate([shifts[pl.ds(s, k3, stride=outs), :] for s in range(outs)], axis=1)
    trace = jnp.concatenate([rec32[pl.ds(s, wrows, stride=outs), :] for s in range(outs)], axis=1)

    qw = zbuf.shape[1] - 128
    slot = pl.ds(pl.multiple_of(me * k3, k3), k3)
    zbuf[slot, 0:k3] = hdot(waves, waves, ((1,), (1,)))
    zbuf[slot, qw : qw + wrows] = hdot(waves, trace, ((1,), (1,)))
    sent_z = exchange("src", me, src_peers, lambda peer: zbuf.at[slot, :], zbuf, k3, zsend, zrecv)
    for copy in sent_z:
        copy.wait()
    both = zbuf[0:k3, :]
    for j in range(1, nsrc):
        both = both + zbuf[j * k3 : (j + 1) * k3, :]
    lane = iota((k3, 128), 1)
    corr = both[:, 0:k3]
    cross = jnp.where(lane < wrows, both[:, qw:], 0.0)

    wide = hdot(pick_rows, corr)
    gram = jnp.zeros((NP, 128), F32)
    shape = (k3, 128)
    row, lane = iota(shape, 0), iota(shape, 1)
    lag = lane - 3 * third(lane)
    for c in range(comps):
        same = ((row >> log_c) == lag) & ((row & (comps - 1)) == c) & (lane < NU)
        grid = hdot(wide, jnp.where(same, 1.0, 0.0).astype(F32)) * hbig[:, c * 128 : (c + 1) * 128]
        for d in range(comps):
            gram = gram + grid[d * NP : (d + 1) * NP]
    spread = hdot(pick_rows, cross) * u_t
    right = jnp.zeros((NP, 128), F32)
    for d in range(comps):
        right = right + spread[d * NP : (d + 1) * NP]
    right = jnp.sum(right, axis=1, keepdims=True)

    damping = float(wrows * total_out * RECV)
    shape = (NP, 128)
    row, lane = iota(shape, 0), iota(shape, 1)
    centre = LAGS_T // 2 * LAGS_X + LAGS_X // 2
    right = right + jnp.where(row == centre, damping, 0.0)
    system = jnp.where(lane == 127, right, gram + jnp.where(row == lane, damping, 0.0))
    for k in range(NU):
        pivot = system[k : k + 1, :] * (1.0 / system[k : k + 1, k : k + 1])
        system = jnp.where(row == k, pivot, system - system[:, k : k + 1] * pivot)
    coef = system[:, 127:128]
    spread = jnp.sum(jnp.where(row == lane, coef, 0.0), axis=0, keepdims=True)
    filt[...] = spread[:, :NU]

    weighted = pick_rows * jnp.concatenate([coef] * comps, axis=0)
    mix = hdot(u_n, weighted)
    matched = hdot(mix, waves)
    t = base + iota((wrows, 1), 0)
    keep = jnp.where((t >= first) & (t < last), 1.0, 0.0).astype(F32)
    prim[...] = ((trace - matched) * keep).astype(BF16)


def solution(mesh):
    nsrc, nfreq = mesh.shape["src"], mesh.shape["freq"]

    def body(data, recip, gap, owner, weights, start_row, end_row, recorded):
        assert data.shape[1] == 1
        wrows, outs, recv = recorded.shape
        comps = 2 * nfreq
        k3 = LAGS_X * comps
        zlanes = -(-k3 // 128) * 128 + 128
        sout = weights.shape[3]
        anywhere = pl.BlockSpec(memory_space=pl.ANY)
        scalar = pl.BlockSpec(memory_space=pltpu.SMEM)
        vmem = pl.BlockSpec(memory_space=pltpu.VMEM)
        dma = pltpu.SemaphoreType.DMA
        primaries, filters = pl.pallas_call(
            functools.partial(kernel, nsrc, nfreq, comps, sout, 1.0 / math.sqrt(nfreq)),
            out_shape=(
                jax.ShapeDtypeStruct((wrows, outs * recv), BF16),
                jax.ShapeDtypeStruct((1, NU), F32),
            ),
            in_specs=[anywhere, anywhere, anywhere, scalar, anywhere, scalar, scalar, anywhere],
            out_specs=(vmem, vmem),
            scratch_shapes=[
                pltpu.VMEM(data.shape, BF16),
                pltpu.VMEM(weights.shape, BF16),
                pltpu.VMEM(recip.shape, BF16),
                pltpu.VMEM(gap.shape, jnp.int32),
                pltpu.VMEM(recorded.shape, BF16),
                pltpu.VMEM((nsrc * 2 * NEAR, recv), BF16),
                pltpu.VMEM((nsrc * 2 * outs, recv), F32),
                pltpu.VMEM((nsrc * 2 * outs, recv), F32),
                pltpu.VMEM((comps * outs, recv), F32),
                pltpu.VMEM((k3 * outs, recv), F32),
                pltpu.VMEM((wrows * outs, recv), F32),
                pltpu.VMEM((nsrc * k3, zlanes), F32),
                pltpu.VMEM((comps * NP, comps * 128), F32),
                dma((3,)),
                dma((2 * CHUNKS,)),
                dma((nsrc,)), dma((nsrc,)),
                dma((nsrc,)), dma((nsrc,)),
                dma((nfreq,)), dma((nfreq,)),
                dma((nsrc,)), dma((nsrc,)),
            ],
            compiler_params=pltpu.CompilerParams(
                collective_id=0, has_side_effects=True, vmem_limit_bytes=56 * 1024 * 1024
            ),
            name="multiples",
        )(data, recip, gap, owner, weights, start_row, end_row, recorded)
        return primaries.reshape(wrows, outs, recv), filters

    placed = (
        P(None, "freq", None, "src"),
        P(None, "freq", None, "src"),
        P(None, "src"),
        P(),
        P(None, "freq", "src", None),
        P("freq"),
        P("freq"),
        P("freq", "src", None),
    )
    return jax.shard_map(
        body,
        mesh=mesh,
        in_specs=placed,
        out_specs=(P("freq", "src", None), P("freq", None)),
        check_vma=False,
    )
```

time: 179 us -> 38.9 us (0.22)
  waiting for transfers between devices: 66.4 us -> 0 us
  blocking collectives: 33 us -> 0 us
  Pallas kernels: 0 us -> 28.7 us
  matrix products: 28.6 us -> 0 us
  between operations: 15.8 us -> 1.93 us
  starting transfers between devices: 12.6 us -> 0 us
  other arithmetic: 12.3 us -> 0 us
    psum x1 -> x0, waiting for transfers between devices: 52.8 us -> none  [body(): summed = lax.psum(jnp.stack([real, imag], axis=1), 'src')]
    pallas_call x0 -> x1, Pallas kernels: none -> 28.7 us  [body(): pl.pallas_call(functools.partial(kernel, nsrc, nfreq, comps, sout, 1.0 /...]
    dot_general x10 -> x0, matrix products: 28.3 us -> none  [the longest x1 8.74 us: body(): matched = jnp.einsum('u,uwsr->wsr', filt, stack, precision=hp)]
    psum x1 -> x0, blocking collectives: 22.4 us -> none  [body(): gram, rhs = lax.psum((gram, rhs), 'src')]
    all_gather x1 -> x0, blocking collectives: 10.7 us -> none  [body(): piece = lax.all_gather(recip, 'src', axis=3, tiled=True)]
    all_to_all x2 -> x0, waiting for transfers between devices: 10.2 us -> none  [the longest x1 5.59 us: body(): lax.all_to_all(local_pred, 'freq', split_axis=3, concat_axis=2, tiled=True)]
    all_to_all x2 -> x0, starting transfers between devices: 7.92 us -> none  [the longest x1 4.6 us: body(): lax.all_to_all(local_pred, 'freq', split_axis=3, concat_axis=2, tiled=True)]
    another operation x6 -> x0, other arithmetic: 6.48 us -> none  [the longest x3 3.13 us: solve_filter(): factor = jnp.linalg.cholesky(gram + damping * eye)]
  transfers between devices with their start and end apart: 5 -> 0, of which waited for: 4 -> 0; matrix products, arithmetic and copies ran while one was open for 0% -> 0% of each run, Pallas kernels for 0% -> 0%
where the time goes in v1:
time: 38.9 us; the launch traced here: 38.6 us
  Pallas kernels  28.7 us (74%)
  local copies, waits for them, and re-layouts  7.94 us (20%)
  between operations  1.93 us (5%)
    pallas_call x1, Pallas kernels, body(): pl.pallas_call(functools.partial(kernel, nsrc, nfreq, comps, sout, 1.0 /...  28.7 us
    unnamed x5, local copies, waits for them, and re-layouts  7.94 us

profile of v1, /device:TPU:0, one launch (start us, length us, event | category | flops | bytes accessed | tf_op | source)
XLA Modules:
  0.0 38.6 jit_solution(12424093228366439518)
XLA Ops:
  1.9 1.4 %copy.10.recip = bf16[2,1,128,16]{3,2,1,0:T(8,128)(2,1)} copy(bf16[2,1,128,16]{2,3,1,0:T(8,128)(2,1)} %param.9) | data formatting | bytes 16384 | tf_op args[1]
  3.4 1.4 %copy.11.gap = s32[128,16]{1,0:T(8,128)} copy(s32[128,16]{0,1:T(8,128)} %param.10) | data formatting | bytes 16384 | tf_op args[2]
  4.8 2.5 %copy.12.weights = bf16[2,1,3072,64]{3,2,1,0:T(8,128)(2,1)} copy(bf16[2,1,3072,64]{2,3,1,0:T(8,128)(2,1)} %param.12) | data formatting | bytes 1572864 | tf_op args[4]
  7.2 28.7 %multiples.1 = (bf16[48,1024]{1,0:T(8,128)(2,1)}, f32[1,27]{1,0:T(1,128)}) custom-call(bf16[2,1,128,3072]{3,2,1,0:T(8,128)(2,1)} %data.1, bf16[2,1,128,16]{3,2,1,0:T(8,128)(2,1)} %copy.10.recip, s32[128,16]{1,0:T(8,128)} %copy.11.gap, s32[8]{0:T(128)} %owner.1, bf16[2,1,3072,64]{3,2,1,0:T(8,128)(2,1)} %copy.12.weights, s32[1]{0:T(128)S(6)} %copy.15.start, ...), custom_call_target="tpu_custom_call" | custom-call | tf_op jit(solution)/shard_map/multiples/pallas_call | solution.py:271
  36.0 1.5 %copy.13 = bf16[6,8,8,128]{3,2,1,0:T(8,128)(2,1)} copy(bf16[6,8,8,128]{3,1,2,0:T(8,128)(2,1)} %bitcast.3) | data formatting | bytes 196608
  37.5 1.1 %copy.17 = f32[1,27]{1,0:T(1,128)} copy(f32[1,27]{1,0:T(1,128)} %get-tuple-element.9) | data formatting | bytes 216

commit v2 on v1

--- a/solution.py
+++ b/solution.py
@@ -34,6 +34,23 @@
 
 def iota(shape, dim):
     return lax.broadcasted_iota(jnp.int32, shape, dim)
+
+
+def split3(x):
+    high = x.astype(BF16).astype(F32)
+    rest = x - high
+    middle = rest.astype(BF16).astype(F32)
+    return high, middle, rest - middle
+
+
+def cosine(turns):
+    y = (turns - NFFT // 2).astype(F32) * (math.pi / NFFT)
+    square = y * y
+    series = jnp.full_like(y, 1.0 / 6227020800.0)
+    for factor in (-1.0 / 39916800.0, 1.0 / 362880.0, -1.0 / 5040.0, 1.0 / 120.0, -1.0 / 6.0, 1.0):
+        series = series * square + factor
+    sine = series * y
+    return 2.0 * sine * sine - 1.0
 
 
 def third(n):
@@ -70,7 +87,7 @@
         big.append(
             (
                 pltpu.make_async_copy(data.at[:, :, :, cut], dbuf.at[:, :, :, cut], dsem.at[2 * i]),
-                pltpu.make_async_copy(weights.at[:, :, cut, :], wbuf.at[:, :, cut, :], dsem.at[2 * i + 1]),
+                pltpu.make_async_copy(weights.at[:, :, :, cut], wbuf.at[:, :, :, cut], dsem.at[2 * i + 1]),
             )
         )
         for copy in big[-1]:
@@ -102,33 +119,28 @@
         return copies
 
     local[0].wait()
-    for i in range(2):
-        flipped = rin[i, 0].astype(F32).T.astype(BF16)
-        rbuf[pl.ds(pl.multiple_of(me * 2 * NEAR + i * NEAR, NEAR), NEAR), :] = flipped
+    mine = pl.ds(pl.multiple_of(me * 2 * NEAR, 2 * NEAR), 2 * NEAR)
+    rbuf[mine, :] = rin[...].reshape(2 * NEAR, RECV)
     pl.semaphore_wait(barrier, nsrc - 1 + nfreq - 1)
-    own = rbuf.at[pl.ds(pl.multiple_of(me * 2 * NEAR, 2 * NEAR), 2 * NEAR), :]
-    sent_r = exchange("src", me, src_peers, lambda peer: own, rbuf, 2 * NEAR, rsend, rrecv)
+    sent_r = exchange("src", me, src_peers, lambda peer: rbuf.at[mine, :], rbuf, 2 * NEAR, rsend, rrecv)
 
     local[1].wait()
-    missing = gin[...] == 1
-    gap_t = jnp.where(missing, 1.0, 0.0).astype(F32).T
-    acc0 = jnp.zeros((2 * RECV, sout), F32)
-    acc1 = jnp.zeros((2 * RECV, sout), F32)
+    gap_t = jnp.where(gin[...] == 1, 1.0, 0.0).astype(F32)
+    present = 1.0 - gap_t.T
+    acc = jnp.zeros((2 * sout, 2 * RECV), F32)
     for i in range(CHUNKS):
         for copy in big[i]:
             copy.wait()
         if i == 0:
             for ci in range(2):
                 head = dbuf[ci, 0, :, :NEAR].astype(F32)
-                dbuf[ci, 0, :, :NEAR] = jnp.where(missing, 0.0, head).astype(BF16)
+                dbuf[ci, 0, :, :NEAR] = jnp.where(present > 0.5, head, 0.0).astype(BF16)
         cut = slice(i * step, (i + 1) * step)
-        left = dbuf[:, 0, :, cut].reshape(2 * RECV, step)
-        acc0 = acc0 + bdot(left, wbuf[0, 0, cut, :])
-        acc1 = acc1 + bdot(left, wbuf[1, 0, cut, :])
-    real = (acc0[:RECV] - acc1[RECV:]).T
-    imag = (acc1[:RECV] + acc0[RECV:]).T
-
-    near_w = [wbuf[ci, 0, :NEAR, :].astype(F32).T.astype(BF16) for ci in range(2)]
+        left = wbuf[:, 0, :, cut].reshape(2 * sout, step)
+        right = dbuf[:, 0, :, cut].reshape(2 * RECV, step)
+        acc = acc + lax.dot_general(left, right, (((1,), (1,)), ((), ())), preferred_element_type=F32)
+
+    near_w = wbuf[:, 0, :, :NEAR].reshape(2 * sout, NEAR)
     for copy in sent_r:
         copy.wait()
     near = []
@@ -138,8 +150,9 @@
             pick = jnp.where(owner[j] == me, 1.0, 0.0).astype(F32)
             total = total + rbuf[j * 2 * NEAR + ci * NEAR : j * 2 * NEAR + (ci + 1) * NEAR, :].astype(F32) * pick
         near.append((total * gap_t).astype(BF16))
-    real = real + bdot(near_w[0], near[0]) - bdot(near_w[1], near[1])
-    imag = imag + bdot(near_w[0], near[1]) + bdot(near_w[1], near[0])
+    acc = acc + bdot(near_w, jnp.concatenate(near, axis=1))
+    real = acc[:sout, :RECV] - acc[sout:, RECV:]
+    imag = acc[sout:, :RECV] + acc[:sout, RECV:]
 
     span = 2 * outs
     for d in range(nsrc):
@@ -161,7 +174,7 @@
         v = t - (third(n) - LAGS_T // 2)
         valid = (t >= first) & (t < last) & (v >= first) & (v < last) & (n < NU)
         turns = ((F_LOW + (c >> 1)) * v + (NFFT // 4) * (c & 1)) & (NFFT - 1)
-        return jnp.where(valid, jnp.cos(turns.astype(F32) * (2.0 * math.pi / NFFT)) * scale, 0.0)
+        return jnp.where(valid, cosine(turns) * scale, 0.0)
 
     rows_cn = comps * NP
     shape = (rows_cn, 128)
@@ -170,18 +183,21 @@
     shape = (wrows, rows_cn)
     lane = iota(shape, 1)
     u_n = delayed(iota(shape, 0), lane >> 5, lane & (NP - 1))
-    shape = (128, 128)
-    for c in range(comps):
-        block = delayed(iota(shape, 0), c, iota(shape, 1))
-        hbig[:, c * 128 : (c + 1) * 128] = hdot(u_t, block)
-    shape = (rows_cn, k3)
+    shape = (rows_cn, 3 * k3)
     row, lane = iota(shape, 0), iota(shape, 1)
+    lane = jnp.where(lane >= 2 * k3, lane - 2 * k3, jnp.where(lane >= k3, lane - k3, lane))
     n = row & (NP - 1)
     same = ((lane >> log_c) == n - 3 * third(n)) & ((lane & (comps - 1)) == (row >> 5)) & (n < NU)
     pick_rows = jnp.where(same, 1.0, 0.0).astype(F32)
+    shape = (k3, rows_cn)
+    row, lane = iota(shape, 0), iota(shape, 1)
+    n = lane & (NP - 1)
+    same = ((row >> log_c) == n - 3 * third(n)) & ((row & (comps - 1)) == (lane >> 5)) & (n < NU)
+    pick_lanes = jnp.where(same, 1.0, 0.0).astype(BF16)
 
     local[2].wait()
     rec32[...] = recb[...].astype(F32).reshape(wrows * outs, RECV)
+    trace = jnp.concatenate([rec32[pl.ds(s, wrows, stride=outs), :] for s in range(outs)], axis=1)
 
     for copy in sent_p:
         copy.wait()
@@ -191,6 +207,7 @@
     mine = pl.ds(pl.multiple_of(here * span, span), span)
     gath[mine, :] = pred
     sent_g = exchange("freq", here, freq_peers, lambda peer: gath.at[mine, :], gath, span, gsend, grecv)
+    hbig[...] = hdot(u_t[:, :wrows], u_n)
     for copy in sent_g:
         copy.wait()
 
@@ -201,36 +218,39 @@
     shifts[size : 2 * size, :] = whole
     shifts[2 * size :, :] = jnp.where(lane == 0, 0.0, pltpu.roll(whole, 1, 1))
     waves = jnp.concatenate([shifts[pl.ds(s, k3, stride=outs), :] for s in range(outs)], axis=1)
-    trace = jnp.concatenate([rec32[pl.ds(s, wrows, stride=outs), :] for s in range(outs)], axis=1)
-
-    qw = zbuf.shape[1] - 128
+
+    parts = split3(waves)
+    stacked = jnp.concatenate([*parts, trace], axis=0).astype(BF16)
+    waves3 = stacked[: 3 * k3]
+    pair = lax.dot_general(waves3, stacked, (((1,), (1,)), ((), ())), preferred_element_type=F32)
+    pair = pair[:k3] + pair[k3 : 2 * k3] + pair[2 * k3 :]
     slot = pl.ds(pl.multiple_of(me * k3, k3), k3)
-    zbuf[slot, 0:k3] = hdot(waves, waves, ((1,), (1,)))
-    zbuf[slot, qw : qw + wrows] = hdot(waves, trace, ((1,), (1,)))
+    zused = 3 * k3 + wrows
+    zbuf[slot, 0:zused] = pair
     sent_z = exchange("src", me, src_peers, lambda peer: zbuf.at[slot, :], zbuf, k3, zsend, zrecv)
     for copy in sent_z:
         copy.wait()
     both = zbuf[0:k3, :]
     for j in range(1, nsrc):
         both = both + zbuf[j * k3 : (j + 1) * k3, :]
-    lane = iota((k3, 128), 1)
-    corr = both[:, 0:k3]
-    cross = jnp.where(lane < wrows, both[:, qw:], 0.0)
-
-    wide = hdot(pick_rows, corr)
-    gram = jnp.zeros((NP, 128), F32)
-    shape = (k3, 128)
-    row, lane = iota(shape, 0), iota(shape, 1)
-    lag = lane - 3 * third(lane)
-    for c in range(comps):
-        same = ((row >> log_c) == lag) & ((row & (comps - 1)) == c) & (lane < NU)
-        grid = hdot(wide, jnp.where(same, 1.0, 0.0).astype(F32)) * hbig[:, c * 128 : (c + 1) * 128]
-        for d in range(comps):
-            gram = gram + grid[d * NP : (d + 1) * NP]
-    spread = hdot(pick_rows, cross) * u_t
-    right = jnp.zeros((NP, 128), F32)
-    for d in range(comps):
+    corr = both[:, 0:k3] + both[:, k3 : 2 * k3] + both[:, 2 * k3 : 3 * k3]
+    cross = both[:, 3 * k3 : zused]
+
+    corr3 = jnp.concatenate(split3(corr), axis=0).astype(BF16)
+    cross3 = jnp.concatenate(split3(cross), axis=0).astype(BF16)
+    pick_bf = pick_rows.astype(BF16)
+    grid = bdot(pick_bf, bdot(corr3, pick_lanes).astype(BF16)) * hbig[...]
+    spread = bdot(pick_bf, cross3) * u_t[:, :wrows]
+    gram = grid[:NP]
+    right = spread[:NP]
+    for d in range(1, comps):
+        gram = gram + grid[d * NP : (d + 1) * NP]
         right = right + spread[d * NP : (d + 1) * NP]
+    tiles = gram[:, :128]
+    for d in range(1, rows_cn // 128):
+        tiles = tiles + gram[:, d * 128 : (d + 1) * 128]
+    tiles = tiles + pltpu.roll(tiles, 64, 1)
+    tiles = tiles + pltpu.roll(tiles, 32, 1)
     right = jnp.sum(right, axis=1, keepdims=True)
 
     damping = float(wrows * total_out * RECV)
@@ -238,17 +258,35 @@
     row, lane = iota(shape, 0), iota(shape, 1)
     centre = LAGS_T // 2 * LAGS_X + LAGS_X // 2
     right = right + jnp.where(row == centre, damping, 0.0)
-    system = jnp.where(lane == 127, right, gram + jnp.where(row == lane, damping, 0.0))
-    for k in range(NU):
-        pivot = system[k : k + 1, :] * (1.0 / system[k : k + 1, k : k + 1])
-        system = jnp.where(row == k, pivot, system - system[:, k : k + 1] * pivot)
+    system = jnp.where(lane == 127, right, tiles + jnp.where(row == lane, damping, 0.0))
+    for k in range(0, NU, 3):
+        cols = [jnp.broadcast_to(system[:, k + i : k + i + 1], (NP, 128)) for i in range(3)]
+        rows = [system[k + i : k + i + 1, :] for i in range(3)]
+        inner = [[cols[j][k + i : k + i + 1, :] for j in range(3)] for i in range(3)]
+        for i in range(3):
+            inverse = 1.0 / inner[i][i]
+            rows[i] = rows[i] * inverse
+            scaled = [None if j <= i else inner[i][j] * inverse for j in range(3)]
+            for j in range(3):
+                if j > i:
+                    rows[j] = rows[j] - inner[j][i] * rows[i]
+                    for m in range(i + 1, 3):
+                        inner[j][m] = inner[j][m] - inner[j][i] * scaled[m]
+            for m in range(i + 1, 3):
+                inner[i][m] = scaled[m]
+        rows[1] = rows[1] - inner[1][2] * rows[2]
+        rows[0] = rows[0] - inner[0][1] * rows[1] - inner[0][2] * rows[2]
+        system = system - (cols[0] * rows[0] + cols[1] * rows[1] + cols[2] * rows[2])
+        for i in range(3):
+            system = jnp.where(row == k + i, rows[i], system)
     coef = system[:, 127:128]
-    spread = jnp.sum(jnp.where(row == lane, coef, 0.0), axis=0, keepdims=True)
-    filt[...] = spread[:, :NU]
+    across = jnp.sum(jnp.where(row == lane, coef, 0.0), axis=0, keepdims=True)
+    filt[...] = across[:, :NU]
 
     weighted = pick_rows * jnp.concatenate([coef] * comps, axis=0)
-    mix = hdot(u_n, weighted)
-    matched = hdot(mix, waves)
+    mix = jnp.concatenate(split3(hdot(u_n, weighted)), axis=0).astype(BF16)
+    matched = bdot(mix, waves3)
+    matched = matched[:wrows] + matched[wrows : 2 * wrows] + matched[2 * wrows :]
     t = base + iota((wrows, 1), 0)
     keep = jnp.where((t >= first) & (t < last), 1.0, 0.0).astype(F32)
     prim[...] = ((trace - matched) * keep).astype(BF16)
@@ -262,8 +300,9 @@
         wrows, outs, recv = recorded.shape
         comps = 2 * nfreq
         k3 = LAGS_X * comps
-        zlanes = -(-k3 // 128) * 128 + 128
-        sout = weights.shape[3]
+        zlanes = -(-(3 * k3 + wrows) // 128) * 128
+        recip, weights, gap = recip.swapaxes(2, 3), weights.swapaxes(2, 3), gap.T
+        sout = weights.shape[2]
         anywhere = pl.BlockSpec(memory_space=pl.ANY)
         scalar = pl.BlockSpec(memory_space=pltpu.SMEM)
         vmem = pl.BlockSpec(memory_space=pltpu.VMEM)
@@ -289,7 +328,7 @@
                 pltpu.VMEM((k3 * outs, recv), F32),
                 pltpu.VMEM((wrows * outs, recv), F32),
                 pltpu.VMEM((nsrc * k3, zlanes), F32),
-                pltpu.VMEM((comps * NP, comps * 128), F32),
+                pltpu.VMEM((comps * NP, comps * NP), F32),
                 dma((3,)),
                 dma((2 * CHUNKS,)),
                 dma((nsrc,)), dma((nsrc,)),

time: 38.9 us -> 28.4 us (0.73)
  local copies, waits for them, and re-layouts: 7.94 us -> 2.74 us
  Pallas kernels: 28.7 us -> 23.5 us
    pallas_call x1, Pallas kernels: 28.7 us -> 23.5 us  [body(): pl.pallas_call(functools.partial(kernel, nsrc, nfreq, comps, sout, 1.0 /...]
    unnamed x5 -> x2, local copies, waits for them, and re-layouts: 7.94 us -> 2.74 us
where the time goes in v2:
time: 28.4 us; the launch traced here: 28.2 us
  Pallas kernels  23.5 us (83%)
  local copies, waits for them, and re-layouts  2.74 us (10%)
  between operations  1.93 us (7%)
    pallas_call x1, Pallas kernels, body(): pl.pallas_call(functools.partial(kernel, nsrc, nfreq, comps, sout, 1.0 /...  23.5 us
    unnamed x2, local copies, waits for them, and re-layouts  2.74 us

profile of v2, /device:TPU:0, one launch (start us, length us, event | category | flops | bytes accessed | tf_op | source)
XLA Modules:
  0.0 28.2 jit_solution(7520838916455649695)
XLA Ops:
  1.9 23.5 %multiples.1 = (bf16[48,1024]{1,0:T(8,128)(2,1)}, f32[1,27]{1,0:T(1,128)}) custom-call(bf16[2,1,128,3072]{3,2,1,0:T(8,128)(2,1)} %data.1, bf16[2,1,16,128]{3,2,1,0:T(8,128)(2,1)} %bitcast.8, s32[16,128]{1,0:T(8,128)} %bitcast.9, s32[8]{0:T(128)} %owner.1, bf16[2,1,64,3072]{3,2,1,0:T(8,128)(2,1)} %bitcast.5, s32[1]{0:T(128)S(6)} %copy.12.start, ...), custom_call_target="tpu_custom_call" | custom-call | tf_op jit(solution)/shard_map/multiples/pallas_call | solution.py:310
  25.4 1.5 %copy.10 = bf16[6,8,8,128]{3,2,1,0:T(8,128)(2,1)} copy(bf16[6,8,8,128]{3,1,2,0:T(8,128)(2,1)} %bitcast.7) | data formatting | bytes 196608
  27.0 1.2 %copy.14 = f32[1,27]{1,0:T(1,128)} copy(f32[1,27]{1,0:T(1,128)} %get-tuple-element.9) | data formatting | bytes 216

commit v3 on v2

--- a/solution.py
+++ b/solution.py
@@ -61,7 +61,7 @@
     nsrc, nfreq, comps, total_out, scale,
     data, recip, gap, owner, weights, start, end, recorded,
     prim, filt,
-    dbuf, wbuf, rin, gin, recb, rbuf, pout, pbuf, gath, shifts, rec32, zbuf, hbig,
+    owner_s, start_s, end_s, dbuf, wbuf, rin, gin, recb, rbuf, pout, pbuf, gath, shifts, rec32, zbuf, hbig,
     lsem, dsem, rsend, rrecv, psend, precv, gsend, grecv, zsend, zrecv,
 ):
     me = lax.axis_index("src")
@@ -78,6 +78,9 @@
         pltpu.make_async_copy(recip, rin, lsem.at[0]),
         pltpu.make_async_copy(gap, gin, lsem.at[1]),
         pltpu.make_async_copy(recorded, recb, lsem.at[2]),
+        pltpu.make_async_copy(owner, owner_s, lsem.at[3]),
+        pltpu.make_async_copy(start, start_s, lsem.at[4]),
+        pltpu.make_async_copy(end, end_s, lsem.at[5]),
     ]
     for copy in local:
         copy.start()
@@ -143,11 +146,12 @@
     near_w = wbuf[:, 0, :, :NEAR].reshape(2 * sout, NEAR)
     for copy in sent_r:
         copy.wait()
+    local[3].wait()
     near = []
     for ci in range(2):
         total = jnp.zeros((NEAR, RECV), F32)
         for j in range(nsrc):
-            pick = jnp.where(owner[j] == me, 1.0, 0.0).astype(F32)
+            pick = jnp.where(owner_s[j] == me, 1.0, 0.0).astype(F32)
             total = total + rbuf[j * 2 * NEAR + ci * NEAR : j * 2 * NEAR + (ci + 1) * NEAR, :].astype(F32) * pick
         near.append((total * gap_t).astype(BF16))
     acc = acc + bdot(near_w, jnp.concatenate(near, axis=1))
@@ -167,7 +171,9 @@
     pbuf[mine, :] = pout[mine, :]
 
     base = here * (wrows - 2 * HALO) - HALO
-    first, last = start[0], end[0]
+    local[4].wait()
+    local[5].wait()
+    first, last = start_s[0], end_s[0]
 
     def delayed(u, c, n):
         t = base + u
@@ -289,7 +295,21 @@
     matched = matched[:wrows] + matched[wrows : 2 * wrows] + matched[2 * wrows :]
     t = base + iota((wrows, 1), 0)
     keep = jnp.where((t >= first) & (t < last), 1.0, 0.0).astype(F32)
-    prim[...] = ((trace - matched) * keep).astype(BF16)
+    result = (trace - matched) * keep
+    for s in range(outs):
+        rec32[pl.ds(s, wrows, stride=outs), :] = result[:, s * RECV : (s + 1) * RECV]
+    prim[...] = rec32[...].astype(BF16)
+
+
+def finish(prim, filt, prim_out, filt_out, sems):
+    copies = [
+        pltpu.make_async_copy(prim, prim_out, sems.at[0]),
+        pltpu.make_async_copy(filt, filt_out, sems.at[1]),
+    ]
+    for copy in copies:
+        copy.start()
+    for copy in copies:
+        copy.wait()
 
 
 def solution(mesh):
@@ -303,19 +323,21 @@
         zlanes = -(-(3 * k3 + wrows) // 128) * 128
         recip, weights, gap = recip.swapaxes(2, 3), weights.swapaxes(2, 3), gap.T
         sout = weights.shape[2]
-        anywhere = pl.BlockSpec(memory_space=pl.ANY)
-        scalar = pl.BlockSpec(memory_space=pltpu.SMEM)
+        anywhere = pl.BlockSpec(memory_space=pltpu.HBM)
         vmem = pl.BlockSpec(memory_space=pltpu.VMEM)
         dma = pltpu.SemaphoreType.DMA
         primaries, filters = pl.pallas_call(
             functools.partial(kernel, nsrc, nfreq, comps, sout, 1.0 / math.sqrt(nfreq)),
             out_shape=(
-                jax.ShapeDtypeStruct((wrows, outs * recv), BF16),
+                jax.ShapeDtypeStruct((wrows * outs, recv), BF16),
                 jax.ShapeDtypeStruct((1, NU), F32),
             ),
-            in_specs=[anywhere, anywhere, anywhere, scalar, anywhere, scalar, scalar, anywhere],
+            in_specs=[anywhere] * 8,
             out_specs=(vmem, vmem),
             scratch_shapes=[
+                pltpu.SMEM(owner.shape, jnp.int32),
+                pltpu.SMEM(start_row.shape, jnp.int32),
+                pltpu.SMEM(end_row.shape, jnp.int32),
                 pltpu.VMEM(data.shape, BF16),
                 pltpu.VMEM(weights.shape, BF16),
                 pltpu.VMEM(recip.shape, BF16),
@@ -329,7 +351,7 @@
                 pltpu.VMEM((wrows * outs, recv), F32),
                 pltpu.VMEM((nsrc * k3, zlanes), F32),
                 pltpu.VMEM((comps * NP, comps * NP), F32),
-                dma((3,)),
+                dma((6,)),
                 dma((2 * CHUNKS,)),
                 dma((nsrc,)), dma((nsrc,)),
                 dma((nsrc,)), dma((nsrc,)),
@@ -341,7 +363,20 @@
             ),
             name="multiples",
         )(data, recip, gap, owner, weights, start_row, end_row, recorded)
-        return primaries.reshape(wrows, outs, recv), filters
+        return tuple(
+            pl.pallas_call(
+                finish,
+                out_shape=(
+                    jax.ShapeDtypeStruct((wrows, outs, recv), BF16),
+                    jax.ShapeDtypeStruct((1, NU), F32),
+                ),
+                in_specs=[anywhere] * 2,
+                out_specs=(anywhere, anywhere),
+                scratch_shapes=[dma((2,))],
+                compiler_params=pltpu.CompilerParams(vmem_limit_bytes=56 * 1024 * 1024),
+                name="finish",
+            )(primaries.reshape(wrows, outs, recv), filters)
+        )
 
     placed = (
         P(None, "freq", None, "src"),

time: 28.4 us -> 28.9 us (1.018)
  Pallas kernels: 23.5 us -> 26.8 us
  local copies, waits for them, and re-layouts: 2.74 us -> 0 us
    pallas_call x0 -> x1, Pallas kernels: none -> 4.11 us  [body(): pl.pallas_call(finish, out_shape=(jax.ShapeDtypeStruct((wrows, outs, recv...]
    unnamed x2 -> x0, local copies, waits for them, and re-layouts: 2.74 us -> none
    pallas_call x1, Pallas kernels: 23.5 us -> 22.7 us  [body(): pl.pallas_call(functools.partial(kernel, nsrc, nfreq, comps, sout, 1.0 /...]
where the time goes in v3:
time: 28.9 us; the launch traced here: 28.8 us
  Pallas kernels  26.8 us (93%)
  between operations  1.93 us (7%)
    pallas_call x1, Pallas kernels, body(): pl.pallas_call(functools.partial(kernel, nsrc, nfreq, comps, sout, 1.0 /...  22.7 us
    pallas_call x1, Pallas kernels, body(): pl.pallas_call(finish, out_shape=(jax.ShapeDtypeStruct((wrows, outs, recv...  4.11 us

profile of v3, /device:TPU:0, one launch (start us, length us, event | category | flops | bytes accessed | tf_op | source)
XLA Modules:
  0.0 28.8 jit_solution(6203375781797063212)
XLA Ops:
  1.9 22.7 %multiples.1 = (bf16[384,128]{1,0:T(8,128)(2,1)}, f32[1,27]{1,0:T(1,128)}) custom-call(bf16[2,1,128,3072]{3,2,1,0:T(8,128)(2,1)} %data.1, bf16[2,1,16,128]{3,2,1,0:T(8,128)(2,1)} %bitcast.6, s32[16,128]{1,0:T(8,128)} %bitcast.7, s32[8]{0:T(128)} %owner.1, bf16[2,1,64,3072]{3,2,1,0:T(8,128)(2,1)} %bitcast.4, s32[1]{0:T(128)S(6)} %copy.10.start, ...), custom_call_target="tpu_custom_call" | custom-call | tf_op jit(solution)/shard_map/multiples/pallas_call | solution.py:329
  24.6 4.1 %finish.1 = (bf16[48,8,128]{2,1,0:T(8,128)(2,1)}, f32[1,27]{1,0:T(1,128)}) custom-call(bf16[48,8,128]{2,1,0:T(8,128)(2,1)} %bitcast.5, f32[1,27]{1,0:T(1,128)} %get-tuple-element.5.filt), custom_call_target="tpu_custom_call" | custom-call | tf_op jit(solution)/shard_map/finish/pallas_call | solution.py:367

commit v4 on v2

--- a/solution.py
+++ b/solution.py
@@ -61,7 +61,7 @@
     nsrc, nfreq, comps, total_out, scale,
     data, recip, gap, owner, weights, start, end, recorded,
     prim, filt,
-    dbuf, wbuf, rin, gin, recb, rbuf, pout, pbuf, gath, shifts, rec32, zbuf, hbig,
+    owner_s, start_s, end_s, dbuf, wbuf, rin, gin, recb, nbuf, nacc, pout, pbuf, gath, shifts, rec32, zbuf, hbig,
     lsem, dsem, rsend, rrecv, psend, precv, gsend, grecv, zsend, zrecv,
 ):
     me = lax.axis_index("src")
@@ -78,6 +78,9 @@
         pltpu.make_async_copy(recip, rin, lsem.at[0]),
         pltpu.make_async_copy(gap, gin, lsem.at[1]),
         pltpu.make_async_copy(recorded, recb, lsem.at[2]),
+        pltpu.make_async_copy(owner, owner_s, lsem.at[3]),
+        pltpu.make_async_copy(start, start_s, lsem.at[4]),
+        pltpu.make_async_copy(end, end_s, lsem.at[5]),
     ]
     for copy in local:
         copy.start()
@@ -118,39 +121,38 @@
             copies[-1].start()
         return copies
 
+    wrow = 3 * NEAR
+    wparts = 2 * sout // 128
+    nrows = wrow + wparts * NEAR
+    at = pl.multiple_of(me * nrows, NEAR)
     local[0].wait()
-    mine = pl.ds(pl.multiple_of(me * 2 * NEAR, 2 * NEAR), 2 * NEAR)
-    rbuf[mine, :] = rin[...].reshape(2 * NEAR, RECV)
-    pl.semaphore_wait(barrier, nsrc - 1 + nfreq - 1)
-    sent_r = exchange("src", me, src_peers, lambda peer: rbuf.at[mine, :], rbuf, 2 * NEAR, rsend, rrecv)
-
+    nbuf[pl.ds(at, 2 * NEAR), :] = rin[...].reshape(2 * NEAR, RECV)
     local[1].wait()
     gap_t = jnp.where(gin[...] == 1, 1.0, 0.0).astype(F32)
+    nbuf[pl.ds(at + 2 * NEAR, NEAR), :] = gap_t.astype(BF16)
     present = 1.0 - gap_t.T
+    for copy in big[0]:
+        copy.wait()
+    near_w = wbuf[:, 0, :, :NEAR].reshape(2 * sout, NEAR).astype(F32)
+    for i in range(wparts):
+        nbuf[pl.ds(at + wrow + i * NEAR, NEAR), :] = near_w[i * 128 : (i + 1) * 128].T.astype(BF16)
+    pl.semaphore_wait(barrier, nsrc - 1 + nfreq - 1)
+    own = nbuf.at[pl.ds(at, nrows), :]
+    sent_r = exchange("src", me, src_peers, lambda peer: own, nbuf, nrows, rsend, rrecv)
+
     acc = jnp.zeros((2 * sout, 2 * RECV), F32)
     for i in range(CHUNKS):
-        for copy in big[i]:
-            copy.wait()
         if i == 0:
             for ci in range(2):
                 head = dbuf[ci, 0, :, :NEAR].astype(F32)
                 dbuf[ci, 0, :, :NEAR] = jnp.where(present > 0.5, head, 0.0).astype(BF16)
+        else:
+            for copy in big[i]:
+                copy.wait()
         cut = slice(i * step, (i + 1) * step)
         left = wbuf[:, 0, :, cut].reshape(2 * sout, step)
         right = dbuf[:, 0, :, cut].reshape(2 * RECV, step)
         acc = acc + lax.dot_general(left, right, (((1,), (1,)), ((), ())), preferred_element_type=F32)
-
-    near_w = wbuf[:, 0, :, :NEAR].reshape(2 * sout, NEAR)
-    for copy in sent_r:
-        copy.wait()
-    near = []
-    for ci in range(2):
-        total = jnp.zeros((NEAR, RECV), F32)
-        for j in range(nsrc):
-            pick = jnp.where(owner[j] == me, 1.0, 0.0).astype(F32)
-            total = total + rbuf[j * 2 * NEAR + ci * NEAR : j * 2 * NEAR + (ci + 1) * NEAR, :].astype(F32) * pick
-        near.append((total * gap_t).astype(BF16))
-    acc = acc + bdot(near_w, jnp.concatenate(near, axis=1))
     real = acc[:sout, :RECV] - acc[sout:, RECV:]
     imag = acc[sout:, :RECV] + acc[:sout, RECV:]
 
@@ -166,8 +168,47 @@
     mine = pl.ds(pl.multiple_of(me * span, span), span)
     pbuf[mine, :] = pout[mine, :]
 
+    local[2].wait()
+    rec32[...] = recb[...].astype(F32).reshape(wrows * outs, RECV)
+    trace = jnp.concatenate([rec32[pl.ds(s, wrows, stride=outs), :] for s in range(outs)], axis=1)
+
+    for copy in sent_r:
+        copy.wait()
+    local[3].wait()
+    fills = []
+    for b in range(nsrc):
+        held = nbuf[b * nrows + 2 * NEAR : b * nrows + 3 * NEAR, :].astype(F32)
+        total = jnp.zeros((2 * NEAR, RECV), F32)
+        for j in range(nsrc):
+            pick = jnp.where(owner_s[j] == b, 1.0, 0.0).astype(F32)
+            total = total + nbuf[j * nrows : j * nrows + 2 * NEAR, :].astype(F32) * pick
+        fills.append(jnp.concatenate([total[:NEAR] * held, total[NEAR:] * held], axis=1).astype(BF16))
+    fill = jnp.concatenate(fills, axis=0)
+    for i in range(wparts):
+        cuts = [b * nrows + wrow + i * NEAR for b in range(nsrc)]
+        left = jnp.concatenate([nbuf[cut : cut + NEAR, :] for cut in cuts], axis=0)
+        nacc[i * 128 : (i + 1) * 128, :] = lax.dot_general(
+            left, fill, (((0,), (0,)), ((), ())), preferred_element_type=F32
+        )
+    by_real = nacc[pl.ds(pl.multiple_of(me * outs, outs), outs), :]
+    by_imag = nacc[pl.ds(pl.multiple_of(sout + me * outs, outs), outs), :]
+    near = jnp.concatenate(
+        [by_real[:, :RECV] - by_imag[:, RECV:], by_imag[:, :RECV] + by_real[:, RECV:]], axis=0
+    )
+
+    for copy in sent_p:
+        copy.wait()
+    pred = near + pbuf[0:span, :]
+    for j in range(1, nsrc):
+        pred = pred + pbuf[j * span : (j + 1) * span, :]
+    mine = pl.ds(pl.multiple_of(here * span, span), span)
+    gath[mine, :] = pred
+    sent_g = exchange("freq", here, freq_peers, lambda peer: gath.at[mine, :], gath, span, gsend, grecv)
+
     base = here * (wrows - 2 * HALO) - HALO
-    first, last = start[0], end[0]
+    local[4].wait()
+    local[5].wait()
+    first, last = start_s[0], end_s[0]
 
     def delayed(u, c, n):
         t = base + u
@@ -183,6 +224,28 @@
     shape = (wrows, rows_cn)
     lane = iota(shape, 1)
     u_n = delayed(iota(shape, 0), lane >> 5, lane & (NP - 1))
+
+    for copy in sent_g:
+        copy.wait()
+
+    size = comps * outs
+    whole = gath[...]
+    lane = iota((size, RECV), 1)
+    shifts[0:size, :] = jnp.where(lane == RECV - 1, 0.0, pltpu.roll(whole, RECV - 1, 1))
+    shifts[size : 2 * size, :] = whole
+    shifts[2 * size :, :] = jnp.where(lane == 0, 0.0, pltpu.roll(whole, 1, 1))
+    waves = jnp.concatenate([shifts[pl.ds(s, k3, stride=outs), :] for s in range(outs)], axis=1)
+
+    parts = split3(waves)
+    stacked = jnp.concatenate([*parts, trace], axis=0).astype(BF16)
+    waves3 = stacked[: 3 * k3]
+    pair = lax.dot_general(waves3, stacked, (((1,), (1,)), ((), ())), preferred_element_type=F32)
+    pair = pair[:k3] + pair[k3 : 2 * k3] + pair[2 * k3 :]
+    slot = pl.ds(pl.multiple_of(me * k3, k3), k3)
+    zused = 3 * k3 + wrows
+    zbuf[slot, 0:zused] = pair
+    sent_z = exchange("src", me, src_peers, lambda peer: zbuf.at[slot, :], zbuf, k3, zsend, zrecv)
+
     shape = (rows_cn, 3 * k3)
     row, lane = iota(shape, 0), iota(shape, 1)
     lane = jnp.where(lane >= 2 * k3, lane - 2 * k3, jnp.where(lane >= k3, lane - k3, lane))
@@ -195,39 +258,7 @@
     same = ((row >> log_c) == n - 3 * third(n)) & ((row & (comps - 1)) == (lane >> 5)) & (n < NU)
     pick_lanes = jnp.where(same, 1.0, 0.0).astype(BF16)
 
-    local[2].wait()
-    rec32[...] = recb[...].astype(F32).reshape(wrows * outs, RECV)
-    trace = jnp.concatenate([rec32[pl.ds(s, wrows, stride=outs), :] for s in range(outs)], axis=1)
-
-    for copy in sent_p:
-        copy.wait()
-    pred = pbuf[0:span, :]
-    for j in range(1, nsrc):
-        pred = pred + pbuf[j * span : (j + 1) * span, :]
-    mine = pl.ds(pl.multiple_of(here * span, span), span)
-    gath[mine, :] = pred
-    sent_g = exchange("freq", here, freq_peers, lambda peer: gath.at[mine, :], gath, span, gsend, grecv)
     hbig[...] = hdot(u_t[:, :wrows], u_n)
-    for copy in sent_g:
-        copy.wait()
-
-    size = comps * outs
-    whole = gath[...]
-    lane = iota((size, RECV), 1)
-    shifts[0:size, :] = jnp.where(lane == RECV - 1, 0.0, pltpu.roll(whole, RECV - 1, 1))
-    shifts[size : 2 * size, :] = whole
-    shifts[2 * size :, :] = jnp.where(lane == 0, 0.0, pltpu.roll(whole, 1, 1))
-    waves = jnp.concatenate([shifts[pl.ds(s, k3, stride=outs), :] for s in range(outs)], axis=1)
-
-    parts = split3(waves)
-    stacked = jnp.concatenate([*parts, trace], axis=0).astype(BF16)
-    waves3 = stacked[: 3 * k3]
-    pair = lax.dot_general(waves3, stacked, (((1,), (1,)), ((), ())), preferred_element_type=F32)
-    pair = pair[:k3] + pair[k3 : 2 * k3] + pair[2 * k3 :]
-    slot = pl.ds(pl.multiple_of(me * k3, k3), k3)
-    zused = 3 * k3 + wrows
-    zbuf[slot, 0:zused] = pair
-    sent_z = exchange("src", me, src_peers, lambda peer: zbuf.at[slot, :], zbuf, k3, zsend, zrecv)
     for copy in sent_z:
         copy.wait()
     both = zbuf[0:k3, :]
@@ -289,7 +320,10 @@
     matched = matched[:wrows] + matched[wrows : 2 * wrows] + matched[2 * wrows :]
     t = base + iota((wrows, 1), 0)
     keep = jnp.where((t >= first) & (t < last), 1.0, 0.0).astype(F32)
-    prim[...] = ((trace - matched) * keep).astype(BF16)
+    result = (trace - matched) * keep
+    for s in range(outs):
+        rec32[pl.ds(s, wrows, stride=outs), :] = result[:, s * RECV : (s + 1) * RECV]
+    prim[...] = rec32[...].astype(BF16)
 
 
 def solution(mesh):
@@ -304,24 +338,27 @@
         recip, weights, gap = recip.swapaxes(2, 3), weights.swapaxes(2, 3), gap.T
         sout = weights.shape[2]
         anywhere = pl.BlockSpec(memory_space=pl.ANY)
-        scalar = pl.BlockSpec(memory_space=pltpu.SMEM)
         vmem = pl.BlockSpec(memory_space=pltpu.VMEM)
         dma = pltpu.SemaphoreType.DMA
         primaries, filters = pl.pallas_call(
             functools.partial(kernel, nsrc, nfreq, comps, sout, 1.0 / math.sqrt(nfreq)),
             out_shape=(
-                jax.ShapeDtypeStruct((wrows, outs * recv), BF16),
+                jax.ShapeDtypeStruct((wrows * outs, recv), BF16),
                 jax.ShapeDtypeStruct((1, NU), F32),
             ),
-            in_specs=[anywhere, anywhere, anywhere, scalar, anywhere, scalar, scalar, anywhere],
+            in_specs=[anywhere] * 8,
             out_specs=(vmem, vmem),
             scratch_shapes=[
+                pltpu.SMEM(owner.shape, jnp.int32),
+                pltpu.SMEM(start_row.shape, jnp.int32),
+                pltpu.SMEM(end_row.shape, jnp.int32),
                 pltpu.VMEM(data.shape, BF16),
                 pltpu.VMEM(weights.shape, BF16),
                 pltpu.VMEM(recip.shape, BF16),
                 pltpu.VMEM(gap.shape, jnp.int32),
                 pltpu.VMEM(recorded.shape, BF16),
-                pltpu.VMEM((nsrc * 2 * NEAR, recv), BF16),
+                pltpu.VMEM((nsrc * (3 * NEAR + 2 * sout // 128 * NEAR), recv), BF16),
+                pltpu.VMEM((2 * sout, 2 * recv), F32),
                 pltpu.VMEM((nsrc * 2 * outs, recv), F32),
                 pltpu.VMEM((nsrc * 2 * outs, recv), F32),
                 pltpu.VMEM((comps * outs, recv), F32),
@@ -329,7 +366,7 @@
                 pltpu.VMEM((wrows * outs, recv), F32),
                 pltpu.VMEM((nsrc * k3, zlanes), F32),
                 pltpu.VMEM((comps * NP, comps * NP), F32),
-                dma((3,)),
+                dma((6,)),
                 dma((2 * CHUNKS,)),
                 dma((nsrc,)), dma((nsrc,)),
                 dma((nsrc,)), dma((nsrc,)),

time: 28.4 us -> 25.8 us (0.908)
  Pallas kernels: 23.5 us -> 20.9 us
    pallas_call x1, Pallas kernels: 23.5 us -> 20.9 us  [body(): pl.pallas_call(functools.partial(kernel, nsrc, nfreq, comps, sout, 1.0 /...]
where the time goes in v4:
time: 25.8 us; the launch traced here: 25.6 us
  Pallas kernels  20.9 us (81%)
  local copies, waits for them, and re-layouts  2.73 us (11%)
  between operations  1.93 us (7%)
    pallas_call x1, Pallas kernels, body(): pl.pallas_call(functools.partial(kernel, nsrc, nfreq, comps, sout, 1.0 /...  20.9 us
    unnamed x2, local copies, waits for them, and re-layouts  2.73 us

profile of v4, /device:TPU:0, one launch (start us, length us, event | category | flops | bytes accessed | tf_op | source)
XLA Modules:
  0.0 25.6 jit_solution(10630740503086097335)
XLA Ops:
  1.9 20.9 %multiples.1 = (bf16[384,128]{1,0:T(8,128)(2,1)}, f32[1,27]{1,0:T(1,128)}) custom-call(bf16[2,1,128,3072]{3,2,1,0:T(8,128)(2,1)} %data.1, bf16[2,1,16,128]{3,2,1,0:T(8,128)(2,1)} %bitcast.6, s32[16,128]{1,0:T(8,128)} %bitcast.7, s32[8]{0:T(128)} %owner.1, bf16[2,1,64,3072]{3,2,1,0:T(8,128)(2,1)} %bitcast.4, s32[1]{0:T(128)S(6)} %copy.12.start, ...), custom_call_target="tpu_custom_call" | custom-call | tf_op jit(solution)/shard_map/multiples/pallas_call | solution.py:343
  22.8 1.5 %copy.14 = bf16[48,8,128]{2,1,0:T(8,128)(2,1)} copy(bf16[48,8,128]{2,1,0:T(8,128)(2,1)} %bitcast.5) | data formatting | bytes 196608
  24.4 1.2 %copy.15 = f32[1,27]{1,0:T(1,128)} copy(f32[1,27]{1,0:T(1,128)} %get-tuple-element.9) | data formatting | bytes 216

commit v5 on v4

--- a/solution.py
+++ b/solution.py
@@ -61,8 +61,8 @@
     nsrc, nfreq, comps, total_out, scale,
     data, recip, gap, owner, weights, start, end, recorded,
     prim, filt,
-    owner_s, start_s, end_s, dbuf, wbuf, rin, gin, recb, nbuf, nacc, pout, pbuf, gath, shifts, rec32, zbuf, hbig,
-    lsem, dsem, rsend, rrecv, psend, precv, gsend, grecv, zsend, zrecv,
+    nbuf, nacc, pout, pbuf, gath, shifts, rec32, zbuf, hbig,
+    rsend, rrecv, psend, precv, gsend, grecv, zsend, zrecv,
 ):
     me = lax.axis_index("src")
     here = lax.axis_index("freq")
@@ -73,28 +73,6 @@
     sout = total_out
     log_c = comps.bit_length() - 1
     k3 = LAGS_X * comps
-
-    local = [
-        pltpu.make_async_copy(recip, rin, lsem.at[0]),
-        pltpu.make_async_copy(gap, gin, lsem.at[1]),
-        pltpu.make_async_copy(recorded, recb, lsem.at[2]),
-        pltpu.make_async_copy(owner, owner_s, lsem.at[3]),
-        pltpu.make_async_copy(start, start_s, lsem.at[4]),
-        pltpu.make_async_copy(end, end_s, lsem.at[5]),
-    ]
-    for copy in local:
-        copy.start()
-    big = []
-    for i in range(CHUNKS):
-        cut = pl.ds(i * step, step)
-        big.append(
-            (
-                pltpu.make_async_copy(data.at[:, :, :, cut], dbuf.at[:, :, :, cut], dsem.at[2 * i]),
-                pltpu.make_async_copy(weights.at[:, :, :, cut], wbuf.at[:, :, :, cut], dsem.at[2 * i + 1]),
-            )
-        )
-        for copy in big[-1]:
-            copy.start()
 
     src_peers = [lax.rem(me + k, nsrc) for k in range(1, nsrc)]
     freq_peers = [lax.rem(here + k, nfreq) for k in range(1, nfreq)]
@@ -125,33 +103,31 @@
     wparts = 2 * sout // 128
     nrows = wrow + wparts * NEAR
     at = pl.multiple_of(me * nrows, NEAR)
-    local[0].wait()
-    nbuf[pl.ds(at, 2 * NEAR), :] = rin[...].reshape(2 * NEAR, RECV)
-    local[1].wait()
-    gap_t = jnp.where(gin[...] == 1, 1.0, 0.0).astype(F32)
+    nbuf[pl.ds(at, 2 * NEAR), :] = recip[...].reshape(2 * NEAR, RECV)
+    gap_t = jnp.where(gap[...] == 1, 1.0, 0.0).astype(F32)
     nbuf[pl.ds(at + 2 * NEAR, NEAR), :] = gap_t.astype(BF16)
     present = 1.0 - gap_t.T
-    for copy in big[0]:
-        copy.wait()
-    near_w = wbuf[:, 0, :, :NEAR].reshape(2 * sout, NEAR).astype(F32)
+    near_w = weights[:, 0, :, :NEAR].reshape(2 * sout, NEAR).astype(F32)
     for i in range(wparts):
         nbuf[pl.ds(at + wrow + i * NEAR, NEAR), :] = near_w[i * 128 : (i + 1) * 128].T.astype(BF16)
     pl.semaphore_wait(barrier, nsrc - 1 + nfreq - 1)
     own = nbuf.at[pl.ds(at, nrows), :]
     sent_r = exchange("src", me, src_peers, lambda peer: own, nbuf, nrows, rsend, rrecv)
 
+    lane = iota((RECV, 128), 1)
+    kept = jnp.concatenate([present] * (128 // NEAR), axis=1)
+    heads = [
+        jnp.where((lane < NEAR) & (kept < 0.5), 0.0, data[ci, 0, :, :128].astype(F32)).astype(BF16)
+        for ci in range(2)
+    ]
+    heads = jnp.concatenate(heads, axis=0)
     acc = jnp.zeros((2 * sout, 2 * RECV), F32)
     for i in range(CHUNKS):
+        cut = slice(i * step, (i + 1) * step)
+        left = weights[:, 0, :, cut].reshape(2 * sout, step)
+        right = data[:, 0, :, cut].reshape(2 * RECV, step)
         if i == 0:
-            for ci in range(2):
-                head = dbuf[ci, 0, :, :NEAR].astype(F32)
-                dbuf[ci, 0, :, :NEAR] = jnp.where(present > 0.5, head, 0.0).astype(BF16)
-        else:
-            for copy in big[i]:
-                copy.wait()
-        cut = slice(i * step, (i + 1) * step)
-        left = wbuf[:, 0, :, cut].reshape(2 * sout, step)
-        right = dbuf[:, 0, :, cut].reshape(2 * RECV, step)
+            right = jnp.concatenate([heads, right[:, 128:]], axis=1)
         acc = acc + lax.dot_general(left, right, (((1,), (1,)), ((), ())), preferred_element_type=F32)
     real = acc[:sout, :RECV] - acc[sout:, RECV:]
     imag = acc[sout:, :RECV] + acc[:sout, RECV:]
@@ -168,19 +144,17 @@
     mine = pl.ds(pl.multiple_of(me * span, span), span)
     pbuf[mine, :] = pout[mine, :]
 
-    local[2].wait()
-    rec32[...] = recb[...].astype(F32).reshape(wrows * outs, RECV)
+    rec32[...] = recorded[...].astype(F32).reshape(wrows * outs, RECV)
     trace = jnp.concatenate([rec32[pl.ds(s, wrows, stride=outs), :] for s in range(outs)], axis=1)
 
     for copy in sent_r:
-        copy.wait()
-    local[3].wait()
+        copy.wait_recv()
     fills = []
     for b in range(nsrc):
         held = nbuf[b * nrows + 2 * NEAR : b * nrows + 3 * NEAR, :].astype(F32)
         total = jnp.zeros((2 * NEAR, RECV), F32)
         for j in range(nsrc):
-            pick = jnp.where(owner_s[j] == b, 1.0, 0.0).astype(F32)
+            pick = jnp.where(owner[j] == b, 1.0, 0.0).astype(F32)
             total = total + nbuf[j * nrows : j * nrows + 2 * NEAR, :].astype(F32) * pick
         fills.append(jnp.concatenate([total[:NEAR] * held, total[NEAR:] * held], axis=1).astype(BF16))
     fill = jnp.concatenate(fills, axis=0)
@@ -197,7 +171,7 @@
     )
 
     for copy in sent_p:
-        copy.wait()
+        copy.wait_recv()
     pred = near + pbuf[0:span, :]
     for j in range(1, nsrc):
         pred = pred + pbuf[j * span : (j + 1) * span, :]
@@ -206,9 +180,7 @@
     sent_g = exchange("freq", here, freq_peers, lambda peer: gath.at[mine, :], gath, span, gsend, grecv)
 
     base = here * (wrows - 2 * HALO) - HALO
-    local[4].wait()
-    local[5].wait()
-    first, last = start_s[0], end_s[0]
+    first, last = start[0], end[0]
 
     def delayed(u, c, n):
         t = base + u
@@ -226,7 +198,7 @@
     u_n = delayed(iota(shape, 0), lane >> 5, lane & (NP - 1))
 
     for copy in sent_g:
-        copy.wait()
+        copy.wait_recv()
 
     size = comps * outs
     whole = gath[...]
@@ -258,9 +230,10 @@
     same = ((row >> log_c) == n - 3 * third(n)) & ((row & (comps - 1)) == (lane >> 5)) & (n < NU)
     pick_lanes = jnp.where(same, 1.0, 0.0).astype(BF16)
 
+    u_parts = jnp.concatenate(split3(u_n), axis=0).astype(BF16)
     hbig[...] = hdot(u_t[:, :wrows], u_n)
     for copy in sent_z:
-        copy.wait()
+        copy.wait_recv()
     both = zbuf[0:k3, :]
     for j in range(1, nsrc):
         both = both + zbuf[j * k3 : (j + 1) * k3, :]
@@ -314,8 +287,12 @@
     across = jnp.sum(jnp.where(row == lane, coef, 0.0), axis=0, keepdims=True)
     filt[...] = across[:, :NU]
 
-    weighted = pick_rows * jnp.concatenate([coef] * comps, axis=0)
-    mix = jnp.concatenate(split3(hdot(u_n, weighted)), axis=0).astype(BF16)
+    mix = jnp.zeros((3 * wrows, 3 * k3), F32)
+    for part in split3(coef):
+        weighted = pick_rows * jnp.concatenate([part] * comps, axis=0)
+        mix = mix + bdot(u_parts, weighted.astype(BF16))
+    mix = mix[:wrows] + mix[wrows : 2 * wrows] + mix[2 * wrows :]
+    mix = jnp.concatenate(split3(mix), axis=0).astype(BF16)
     matched = bdot(mix, waves3)
     matched = matched[:wrows] + matched[wrows : 2 * wrows] + matched[2 * wrows :]
     t = base + iota((wrows, 1), 0)
@@ -324,6 +301,13 @@
     for s in range(outs):
         rec32[pl.ds(s, wrows, stride=outs), :] = result[:, s * RECV : (s + 1) * RECV]
     prim[...] = rec32[...].astype(BF16)
+    for copy in sent_r + sent_p + sent_g + sent_z:
+        copy.wait_send()
+
+
+def finish(prim, filt, prim_out, filt_out):
+    prim_out[...] = prim[...]
+    filt_out[...] = filt[...]
 
 
 def solution(mesh):
@@ -337,7 +321,8 @@
         zlanes = -(-(3 * k3 + wrows) // 128) * 128
         recip, weights, gap = recip.swapaxes(2, 3), weights.swapaxes(2, 3), gap.T
         sout = weights.shape[2]
-        anywhere = pl.BlockSpec(memory_space=pl.ANY)
+        scalar = pl.BlockSpec(memory_space=pltpu.SMEM)
+        limit = 16 * 1024 * 1024 + 8 * 4 * (comps * NP) ** 2
         vmem = pl.BlockSpec(memory_space=pltpu.VMEM)
         dma = pltpu.SemaphoreType.DMA
         primaries, filters = pl.pallas_call(
@@ -346,17 +331,9 @@
                 jax.ShapeDtypeStruct((wrows * outs, recv), BF16),
                 jax.ShapeDtypeStruct((1, NU), F32),
             ),
-            in_specs=[anywhere] * 8,
+            in_specs=[vmem, vmem, vmem, scalar, vmem, scalar, scalar, vmem],
             out_specs=(vmem, vmem),
             scratch_shapes=[
-                pltpu.SMEM(owner.shape, jnp.int32),
-                pltpu.SMEM(start_row.shape, jnp.int32),
-                pltpu.SMEM(end_row.shape, jnp.int32),
-                pltpu.VMEM(data.shape, BF16),
-                pltpu.VMEM(weights.shape, BF16),
-                pltpu.VMEM(recip.shape, BF16),
-                pltpu.VMEM(gap.shape, jnp.int32),
-                pltpu.VMEM(recorded.shape, BF16),
                 pltpu.VMEM((nsrc * (3 * NEAR + 2 * sout // 128 * NEAR), recv), BF16),
                 pltpu.VMEM((2 * sout, 2 * recv), F32),
                 pltpu.VMEM((nsrc * 2 * outs, recv), F32),
@@ -366,19 +343,28 @@
                 pltpu.VMEM((wrows * outs, recv), F32),
                 pltpu.VMEM((nsrc * k3, zlanes), F32),
                 pltpu.VMEM((comps * NP, comps * NP), F32),
-                dma((6,)),
-                dma((2 * CHUNKS,)),
                 dma((nsrc,)), dma((nsrc,)),
                 dma((nsrc,)), dma((nsrc,)),
                 dma((nfreq,)), dma((nfreq,)),
                 dma((nsrc,)), dma((nsrc,)),
             ],
             compiler_params=pltpu.CompilerParams(
-                collective_id=0, has_side_effects=True, vmem_limit_bytes=56 * 1024 * 1024
+                collective_id=0, has_side_effects=True, vmem_limit_bytes=limit
             ),
             name="multiples",
         )(data, recip, gap, owner, weights, start_row, end_row, recorded)
-        return primaries.reshape(wrows, outs, recv), filters
+        return tuple(
+            pl.pallas_call(
+                finish,
+                out_shape=(
+                    jax.ShapeDtypeStruct((wrows, outs, recv), BF16),
+                    jax.ShapeDtypeStruct((1, NU), F32),
+                ),
+                in_specs=[vmem] * 2,
+                out_specs=(vmem, vmem),
+                name="finish",
+            )(primaries.reshape(wrows, outs, recv), filters)
+        )
 
     placed = (
         P(None, "freq", None, "src"),

time: 25.8 us -> 31.2 us (1.21)
  local copies, waits for them, and re-layouts: 2.73 us -> 6.64 us
  Pallas kernels: 20.9 us -> 22.2 us
    unnamed x2 -> x16, local copies, waits for them, and re-layouts: 2.73 us -> 6.64 us
    pallas_call x0 -> x1, Pallas kernels: none -> 1.54 us  [body(): pl.pallas_call(finish, out_shape=(jax.ShapeDtypeStruct((wrows, outs, recv...]
where the time goes in v5:
time: 31.2 us; the launch traced here: 30.8 us
  Pallas kernels  22.2 us (71%)
  local copies, waits for them, and re-layouts  6.64 us (21%)
  between operations  1.95 us (6%)
    pallas_call x1, Pallas kernels, body(): pl.pallas_call(functools.partial(kernel, nsrc, nfreq, comps, sout, 1.0 /...  20.7 us
    unnamed x16, local copies, waits for them, and re-layouts  6.64 us
    pallas_call x1, Pallas kernels, body(): pl.pallas_call(finish, out_shape=(jax.ShapeDtypeStruct((wrows, outs, recv...  1.54 us

profile of v5, /device:TPU:0, one launch (start us, length us, event | category | flops | bytes accessed | tf_op | source)
XLA Modules:
  0.0 30.8 jit_solution(2378810810352846754)
XLA Ops:
  1.9 0.0 copy-start
  1.9 1.4 %copy-done = bf16[2,1,128,3072]{3,2,1,0:T(8,128)(2,1)S(1)} copy-done((bf16[2,1,128,3072]{3,2,1,0:T(8,128)(2,1)S(1)}, bf16[2,1,128,3072]{3,2,1,0:T(8,128)(2,1)}, u32[]{:S(2)}) %copy-start) | copy-done | bytes 1572888
  3.3 0.0 copy-start.1
  3.3 1.1 %copy-done.1 = bf16[2,1,3072,64]{2,3,1,0:T(8,128)(2,1)S(1)} copy-done((bf16[2,1,3072,64]{2,3,1,0:T(8,128)(2,1)S(1)}, bf16[2,1,3072,64]{2,3,1,0:T(8,128)(2,1)}, u32[]{:S(2)}) %copy-start.1) | copy-done | bytes 786456
  4.5 0.0 copy-start.2
  4.5 0.9 %copy-done.2 = bf16[48,8,128]{2,1,0:T(8,128)(2,1)S(1)} copy-done((bf16[48,8,128]{2,1,0:T(8,128)(2,1)S(1)}, bf16[48,8,128]{2,1,0:T(8,128)(2,1)}, u32[]{:S(2)}) %copy-start.2) | copy-done | bytes 98328
  5.4 0.0 copy-start.4
  5.4 0.7 %copy-done.4 = bf16[2,1,128,16]{2,3,1,0:T(8,128)(2,1)S(1)} copy-done((bf16[2,1,128,16]{2,3,1,0:T(8,128)(2,1)S(1)}, bf16[2,1,128,16]{2,3,1,0:T(8,128)(2,1)}, u32[]{:S(2)}) %copy-start.4) | copy-done | bytes 8216
  6.1 0.0 copy-start.5
  6.1 0.7 %copy-done.5 = s32[128,16]{0,1:T(8,128)S(1)} copy-done((s32[128,16]{0,1:T(8,128)S(1)}, s32[128,16]{0,1:T(8,128)}, u32[]{:S(2)}) %copy-start.5) | copy-done | bytes 8216
  6.8 0.0 copy-start.6
  6.8 0.7 %copy-done.6 = s32[8]{0:T(128)S(1)} copy-done((s32[8]{0:T(128)S(1)}, s32[8]{0:T(128)}, u32[]{:S(2)}) %copy-start.6) | copy-done | bytes 56
  7.4 20.7 %multiples.1 = (bf16[384,128]{1,0:T(8,128)(2,1)S(1)}, f32[1,27]{1,0:T(1,128)S(1)}) custom-call(bf16[2,1,128,3072]{3,2,1,0:T(8,128)(2,1)S(1)} %copy-done, bf16[2,1,16,128]{3,2,1,0:T(8,128)(2,1)S(1)} %bitcast.6, s32[16,128]{1,0:T(8,128)S(1)} %bitcast.7, s32[8]{0:T(128)S(1)} %copy-done.6, bf16[2,1,64,3072]{3,2,1,0:T(8,128)(2,1)S(1)} %bitcast.4, ...), custom_call_target="tpu_custom_call" | custom-call | tf_op jit(solution)/shard_map/multiples/pallas_call | solution.py:328
  28.1 0.0 copy-start.3
  28.1 0.6 %copy-done.3 = bf16[384,128]{1,0:T(8,128)(2,1)} copy-done((bf16[384,128]{1,0:T(8,128)(2,1)}, bf16[384,128]{1,0:T(8,128)(2,1)S(1)}, u32[]{:S(2)}) %copy-start.3) | copy-done | bytes 98328
  28.7 0.0 copy-start.7
  28.7 0.5 %copy-done.7 = f32[1,27]{1,0:T(1,128)} copy-done((f32[1,27]{1,0:T(1,128)}, f32[1,27]{1,0:T(1,128)S(1)}, u32[]{:S(2)}) %copy-start.7) | copy-done | bytes 132
  29.3 1.5 %finish.1 = (bf16[48,8,128]{2,1,0:T(8,128)(2,1)}, f32[1,27]{1,0:T(1,128)}) custom-call(bf16[48,8,128]{2,1,0:T(8,128)(2,1)} %bitcast.5, f32[1,27]{1,0:T(1,128)} %copy-done.7), custom_call_target="tpu_custom_call" | custom-call | tf_op jit(solution)/shard_map/finish/pallas_call | solution.py:357
Async XLA Ops:
  1.9 1.4 %copy-start = (bf16[2,1,128,3072]{3,2,1,0:T(8,128)(2,1)S(1)}, bf16[2,1,128,3072]{3,2,1,0:T(8,128)(2,1)}, u32[]{:S(2)}) copy-start(bf16[2,1,128,3072]{3,2,1,0:T(8,128)(2,1)} %data.1) | copy-start | bytes 4718596
  3.3 1.1 %copy-start.1 = (bf16[2,1,3072,64]{2,3,1,0:T(8,128)(2,1)S(1)}, bf16[2,1,3072,64]{2,3,1,0:T(8,128)(2,1)}, u32[]{:S(2)}) copy-start(bf16[2,1,3072,64]{2,3,1,0:T(8,128)(2,1)} %param.12) | copy-start | bytes 2359300
  4.5 0.9 %copy-start.2 = (bf16[48,8,128]{2,1,0:T(8,128)(2,1)S(1)}, bf16[48,8,128]{2,1,0:T(8,128)(2,1)}, u32[]{:S(2)}) copy-start(bf16[48,8,128]{2,1,0:T(8,128)(2,1)} %recorded.1) | copy-start | bytes 294916
  5.4 0.7 %copy-start.4 = (bf16[2,1,128,16]{2,3,1,0:T(8,128)(2,1)S(1)}, bf16[2,1,128,16]{2,3,1,0:T(8,128)(2,1)}, u32[]{:S(2)}) copy-start(bf16[2,1,128,16]{2,3,1,0:T(8,128)(2,1)} %param.9) | copy-start | bytes 24580
  6.1 0.7 %copy-start.5 = (s32[128,16]{0,1:T(8,128)S(1)}, s32[128,16]{0,1:T(8,128)}, u32[]{:S(2)}) copy-start(s32[128,16]{0,1:T(8,128)} %param.10) | copy-start | bytes 24580
  6.8 0.7 %copy-start.6 = (s32[8]{0:T(128)S(1)}, s32[8]{0:T(128)}, u32[]{:S(2)}) copy-start(s32[8]{0:T(128)} %owner.1) | copy-start | bytes 100
  28.1 0.6 %copy-start.3 = (bf16[384,128]{1,0:T(8,128)(2,1)}, bf16[384,128]{1,0:T(8,128)(2,1)S(1)}, u32[]{:S(2)}) copy-start(bf16[384,128]{1,0:T(8,128)(2,1)S(1)} %get-tuple-element.4) | copy-start | bytes 294916
  28.7 0.5 %copy-start.7 = (f32[1,27]{1,0:T(1,128)}, f32[1,27]{1,0:T(1,128)S(1)}, u32[]{:S(2)}) copy-start(f32[1,27]{1,0:T(1,128)S(1)} %get-tuple-element.5.filt) | copy-start | bytes 328

commit v6 on v4

--- a/solution.py
+++ b/solution.py
@@ -140,7 +140,7 @@
     own = nbuf.at[pl.ds(at, nrows), :]
     sent_r = exchange("src", me, src_peers, lambda peer: own, nbuf, nrows, rsend, rrecv)
 
-    acc = jnp.zeros((2 * sout, 2 * RECV), F32)
+    acc = jnp.zeros((2 * RECV, 2 * sout), F32)
     for i in range(CHUNKS):
         if i == 0:
             for ci in range(2):
@@ -152,7 +152,8 @@
         cut = slice(i * step, (i + 1) * step)
         left = wbuf[:, 0, :, cut].reshape(2 * sout, step)
         right = dbuf[:, 0, :, cut].reshape(2 * RECV, step)
-        acc = acc + lax.dot_general(left, right, (((1,), (1,)), ((), ())), preferred_element_type=F32)
+        acc = acc + lax.dot_general(right, left, (((1,), (1,)), ((), ())), preferred_element_type=F32)
+    acc = acc.T
     real = acc[:sout, :RECV] - acc[sout:, RECV:]
     imag = acc[sout:, :RECV] + acc[:sout, RECV:]
 
@@ -173,7 +174,7 @@
     trace = jnp.concatenate([rec32[pl.ds(s, wrows, stride=outs), :] for s in range(outs)], axis=1)
 
     for copy in sent_r:
-        copy.wait()
+        copy.wait_recv()
     local[3].wait()
     fills = []
     for b in range(nsrc):
@@ -197,7 +198,7 @@
     )
 
     for copy in sent_p:
-        copy.wait()
+        copy.wait_recv()
     pred = near + pbuf[0:span, :]
     for j in range(1, nsrc):
         pred = pred + pbuf[j * span : (j + 1) * span, :]
@@ -226,7 +227,7 @@
     u_n = delayed(iota(shape, 0), lane >> 5, lane & (NP - 1))
 
     for copy in sent_g:
-        copy.wait()
+        copy.wait_recv()
 
     size = comps * outs
     whole = gath[...]
@@ -258,9 +259,10 @@
     same = ((row >> log_c) == n - 3 * third(n)) & ((row & (comps - 1)) == (lane >> 5)) & (n < NU)
     pick_lanes = jnp.where(same, 1.0, 0.0).astype(BF16)
 
+    u_parts = jnp.concatenate(split3(u_n), axis=0).astype(BF16)
     hbig[...] = hdot(u_t[:, :wrows], u_n)
     for copy in sent_z:
-        copy.wait()
+        copy.wait_recv()
     both = zbuf[0:k3, :]
     for j in range(1, nsrc):
         both = both + zbuf[j * k3 : (j + 1) * k3, :]
@@ -314,8 +316,12 @@
     across = jnp.sum(jnp.where(row == lane, coef, 0.0), axis=0, keepdims=True)
     filt[...] = across[:, :NU]
 
-    weighted = pick_rows * jnp.concatenate([coef] * comps, axis=0)
-    mix = jnp.concatenate(split3(hdot(u_n, weighted)), axis=0).astype(BF16)
+    mix = jnp.zeros((3 * wrows, 3 * k3), F32)
+    for part in split3(coef):
+        weighted = pick_rows * jnp.concatenate([part] * comps, axis=0)
+        mix = mix + bdot(u_parts, weighted.astype(BF16))
+    mix = mix[:wrows] + mix[wrows : 2 * wrows] + mix[2 * wrows :]
+    mix = jnp.concatenate(split3(mix), axis=0).astype(BF16)
     matched = bdot(mix, waves3)
     matched = matched[:wrows] + matched[wrows : 2 * wrows] + matched[2 * wrows :]
     t = base + iota((wrows, 1), 0)
@@ -324,6 +330,13 @@
     for s in range(outs):
         rec32[pl.ds(s, wrows, stride=outs), :] = result[:, s * RECV : (s + 1) * RECV]
     prim[...] = rec32[...].astype(BF16)
+    for copy in sent_r + sent_p + sent_g + sent_z:
+        copy.wait_send()
+
+
+def finish(prim, filt, prim_out, filt_out):
+    prim_out[...] = prim[...]
+    filt_out[...] = filt[...]
 
 
 def solution(mesh):
@@ -378,7 +391,19 @@
             ),
             name="multiples",
         )(data, recip, gap, owner, weights, start_row, end_row, recorded)
-        return primaries.reshape(wrows, outs, recv), filters
+        return tuple(
+            pl.pallas_call(
+                finish,
+                out_shape=(
+                    jax.ShapeDtypeStruct((wrows, outs, recv), BF16),
+                    jax.ShapeDtypeStruct((1, NU), F32),
+                ),
+                in_specs=[vmem] * 2,
+                out_specs=(vmem, vmem),
+                compiler_params=pltpu.CompilerParams(vmem_limit_bytes=56 * 1024 * 1024),
+                name="finish",
+            )(primaries.reshape(wrows, outs, recv), filters)
+        )
 
     placed = (
         P(None, "freq", None, "src"),

time: 25.8 us -> 24.6 us (0.953)
  local copies, waits for them, and re-layouts: 2.73 us -> 0 us
  Pallas kernels: 20.9 us -> 22.5 us
    unnamed x2 -> x0, local copies, waits for them, and re-layouts: 2.73 us -> none
    pallas_call x0 -> x1, Pallas kernels: none -> 1.55 us  [body(): pl.pallas_call(finish, out_shape=(jax.ShapeDtypeStruct((wrows, outs, recv...]
where the time goes in v6:
time: 24.6 us; the launch traced here: 24.4 us
  Pallas kernels  22.5 us (91%)
  between operations  1.93 us (8%)
    pallas_call x1, Pallas kernels, body(): pl.pallas_call(functools.partial(kernel, nsrc, nfreq, comps, sout, 1.0 /...  20.9 us
    pallas_call x1, Pallas kernels, body(): pl.pallas_call(finish, out_shape=(jax.ShapeDtypeStruct((wrows, outs, recv...  1.55 us

profile of v6, /device:TPU:0, one launch (start us, length us, event | category | flops | bytes accessed | tf_op | source)
XLA Modules:
  0.0 24.4 jit_solution(8607104309683662494)
XLA Ops:
  1.9 20.9 %multiples.1 = (bf16[384,128]{1,0:T(8,128)(2,1)}, f32[1,27]{1,0:T(1,128)}) custom-call(bf16[2,1,128,3072]{3,2,1,0:T(8,128)(2,1)} %data.1, bf16[2,1,16,128]{3,2,1,0:T(8,128)(2,1)} %bitcast.6, s32[16,128]{1,0:T(8,128)} %bitcast.7, s32[8]{0:T(128)} %owner.1, bf16[2,1,64,3072]{3,2,1,0:T(8,128)(2,1)} %bitcast.4, s32[1]{0:T(128)S(6)} %copy.10.start, ...), custom_call_target="tpu_custom_call" | custom-call | tf_op jit(solution)/shard_map/multiples/pallas_call | solution.py:356
  22.9 1.5 %finish.1 = (bf16[48,8,128]{2,1,0:T(8,128)(2,1)}, f32[1,27]{1,0:T(1,128)}) custom-call(bf16[48,8,128]{2,1,0:T(8,128)(2,1)} %bitcast.5, f32[1,27]{1,0:T(1,128)} %get-tuple-element.5.filt), custom_call_target="tpu_custom_call" | custom-call | tf_op jit(solution)/shard_map/finish/pallas_call | solution.py:395

commit v7 on v6

--- a/solution.py
+++ b/solution.py
@@ -55,6 +55,24 @@
 
 def third(n):
     return (n * 171) >> 9
+
+
+def partners(index, count):
+    if count & (count - 1):
+        return [lax.rem(index + k, count) for k in range(1, count)]
+    found = []
+    for flips in range(count - 1, 0, -1):
+        peer = 0
+        for bit in range(count.bit_length() - 1):
+            value = 1 << bit
+            peer = peer + lax.rem(lax.div(index, value) + (flips >> bit) % 2, 2) * value
+        found.append(peer)
+    return found
+
+
+def inverse_of(x):
+    guess = pl.reciprocal(x, approx=True)
+    return guess * (2.0 - x * guess)
 
 
 def kernel(
@@ -96,8 +114,8 @@
         for copy in big[-1]:
             copy.start()
 
-    src_peers = [lax.rem(me + k, nsrc) for k in range(1, nsrc)]
-    freq_peers = [lax.rem(here + k, nfreq) for k in range(1, nfreq)]
+    src_peers = partners(me, nsrc)
+    freq_peers = partners(here, nfreq)
     barrier = pltpu.get_barrier_semaphore()
     for peer in src_peers:
         pl.semaphore_signal(barrier, inc=1, device_id={"src": peer}, device_id_type=pl.DeviceIdType.MESH)
@@ -297,7 +315,7 @@
         rows = [system[k + i : k + i + 1, :] for i in range(3)]
         inner = [[cols[j][k + i : k + i + 1, :] for j in range(3)] for i in range(3)]
         for i in range(3):
-            inverse = 1.0 / inner[i][i]
+            inverse = inverse_of(inner[i][i])
             rows[i] = rows[i] * inverse
             scaled = [None if j <= i else inner[i][j] * inverse for j in range(3)]
             for j in range(3):

time: 24.6 us -> 24.8 us (level)
  no operation moved by 1% of the time
where the time goes in v7:
time: 24.8 us; the launch traced here: 24.6 us
  Pallas kernels  22.7 us (92%)
  between operations  1.93 us (8%)
    pallas_call x1, Pallas kernels, body(): pl.pallas_call(functools.partial(kernel, nsrc, nfreq, comps, sout, 1.0 /...  21.2 us
    pallas_call x1, Pallas kernels, body(): pl.pallas_call(finish, out_shape=(jax.ShapeDtypeStruct((wrows, outs, recv...  1.55 us

profile of v7, /device:TPU:0, one launch (start us, length us, event | category | flops | bytes accessed | tf_op | source)
XLA Modules:
  0.0 24.6 jit_solution(2697079122833432956)
XLA Ops:
  1.9 21.2 %multiples.1 = (bf16[384,128]{1,0:T(8,128)(2,1)}, f32[1,27]{1,0:T(1,128)}) custom-call(bf16[2,1,128,3072]{3,2,1,0:T(8,128)(2,1)} %data.1, bf16[2,1,16,128]{3,2,1,0:T(8,128)(2,1)} %bitcast.6, s32[16,128]{1,0:T(8,128)} %bitcast.7, s32[8]{0:T(128)} %owner.1, bf16[2,1,64,3072]{3,2,1,0:T(8,128)(2,1)} %bitcast.4, s32[1]{0:T(128)S(6)} %copy.10.start, ...), custom_call_target="tpu_custom_call" | custom-call | tf_op jit(solution)/shard_map/multiples/pallas_call | solution.py:374
  23.1 1.5 %finish.1 = (bf16[48,8,128]{2,1,0:T(8,128)(2,1)}, f32[1,27]{1,0:T(1,128)}) custom-call(bf16[48,8,128]{2,1,0:T(8,128)(2,1)} %bitcast.5, f32[1,27]{1,0:T(1,128)} %get-tuple-element.5.filt), custom_call_target="tpu_custom_call" | custom-call | tf_op jit(solution)/shard_map/finish/pallas_call | solution.py:413

commit v8 on v6

--- a/solution.py
+++ b/solution.py
@@ -55,6 +55,11 @@
 
 def third(n):
     return (n * 171) >> 9
+
+
+def inverse_of(x):
+    guess = pl.reciprocal(x, approx=True)
+    return guess * (2.0 - x * guess)
 
 
 def kernel(
@@ -297,7 +302,7 @@
         rows = [system[k + i : k + i + 1, :] for i in range(3)]
         inner = [[cols[j][k + i : k + i + 1, :] for j in range(3)] for i in range(3)]
         for i in range(3):
-            inverse = 1.0 / inner[i][i]
+            inverse = inverse_of(inner[i][i])
             rows[i] = rows[i] * inverse
             scaled = [None if j <= i else inner[i][j] * inverse for j in range(3)]
             for j in range(3):

time: 24.6 us -> 24.8 us (level)
  no operation moved by 1% of the time
where the time goes in v8:
time: 24.8 us; the launch traced here: 24.6 us
  Pallas kernels  22.7 us (92%)
  between operations  1.93 us (8%)
    pallas_call x1, Pallas kernels, body(): pl.pallas_call(functools.partial(kernel, nsrc, nfreq, comps, sout, 1.0 /...  21.1 us
    pallas_call x1, Pallas kernels, body(): pl.pallas_call(finish, out_shape=(jax.ShapeDtypeStruct((wrows, outs, recv...  1.55 us

profile of v8, /device:TPU:0, one launch (start us, length us, event | category | flops | bytes accessed | tf_op | source)
XLA Modules:
  0.0 24.6 jit_solution(15237010557525829402)
XLA Ops:
  1.9 21.1 %multiples.1 = (bf16[384,128]{1,0:T(8,128)(2,1)}, f32[1,27]{1,0:T(1,128)}) custom-call(bf16[2,1,128,3072]{3,2,1,0:T(8,128)(2,1)} %data.1, bf16[2,1,16,128]{3,2,1,0:T(8,128)(2,1)} %bitcast.6, s32[16,128]{1,0:T(8,128)} %bitcast.7, s32[8]{0:T(128)} %owner.1, bf16[2,1,64,3072]{3,2,1,0:T(8,128)(2,1)} %bitcast.4, s32[1]{0:T(128)S(6)} %copy.10.start, ...), custom_call_target="tpu_custom_call" | custom-call | tf_op jit(solution)/shard_map/multiples/pallas_call | solution.py:361
  23.1 1.5 %finish.1 = (bf16[48,8,128]{2,1,0:T(8,128)(2,1)}, f32[1,27]{1,0:T(1,128)}) custom-call(bf16[48,8,128]{2,1,0:T(8,128)(2,1)} %bitcast.5, f32[1,27]{1,0:T(1,128)} %get-tuple-element.5.filt), custom_call_target="tpu_custom_call" | custom-call | tf_op jit(solution)/shard_map/finish/pallas_call | solution.py:400
